TPU v7x, 128 devices: a whole 4x4x4 slice. The times are simulated.
128 devices in a mesh: rep: 8 (over x, core), shard: 16 (over z, y).
Axes of the slice: x: 4, y: 4, z: 4, core: 2. Of those that a mesh axis runs over, the one named last changes fastest.
Arguments:
- tokens: bfloat16 [16384, 768], P(('rep', 'shard')), may hold values from -6 to 6
- segments: int32 [16384], P(('rep', 'shard')), may hold values from 0 to 23, as said below
- w_qkv: bfloat16 [768, 2304], P('shard'), may hold values from -0.21875 to 0.21875
- w_out: bfloat16 [768, 768], P('shard'), may hold values from -0.875 to 0.875
- w_up: bfloat16 [768, 3072], P('shard'), may hold values from -0.21875 to 0.21875
- w_down: bfloat16 [3072, 768], P('shard'), may hold values from -0.109375 to 0.109375
- b_query: bfloat16 [768], P('shard'), may hold values from -3 to 3
- b_value: bfloat16 [768], P('shard'), may hold values from -3 to 3
- b_out: bfloat16 [768], P('shard'), may hold values from -3 to 3
- b_up: bfloat16 [3072], P('shard'), may hold values from -3 to 3
- b_down: bfloat16 [768], P('shard'), may hold values from -3 to 3
- ln1_gain: bfloat16 [768], P('shard'), may hold values from 0.5 to 1.5
- ln1_shift: bfloat16 [768], P('shard'), may hold values from -2 to 2
- ln2_gain: bfloat16 [768], P('shard'), may hold values from 0.5 to 1.5
- ln2_shift: bfloat16 [768], P('shard'), may hold values from -2 to 2
- cotangent: bfloat16 [16384, 768], P(('rep', 'shard')), may hold values from -6 to 6
Outputs:
- out_tokens: bfloat16 [16384, 768], P(('rep', 'shard'))
- d_tokens: bfloat16 [16384, 768], P(('rep', 'shard'))
- d_w_qkv: float32 [768, 2304], P('shard')
- d_w_out: float32 [768, 768], P('shard')
- d_w_up: float32 [768, 3072], P('shard')
- d_w_down: float32 [3072, 768], P('shard')
- d_b_query: float32 [768], P('shard')
- d_b_value: float32 [768], P('shard')
- d_b_out: float32 [768], P('shard')
- d_b_up: float32 [3072], P('shard')
- d_b_down: float32 [768], P('shard')
- d_ln1_gain: float32 [768], P('shard')
- d_ln1_shift: float32 [768], P('shard')
- d_ln2_gain: float32 [768], P('shard')
- d_ln2_shift: float32 [768], P('shard')
Inputs may be any that keep to these rules, and one draw needn't show every extreme that they name: `segments`: numbers never fall along the tokens. The 2048 tokens of replica group r carry the numbers 3 r, 3 r + 1 and 3 r + 2; the middle document starts on a token of the group's first 128 and ends on one of its last 128, and the other two are shorter than 128 tokens.
All inputs are finite; a program needn't handle non-finite values.
Results may differ from a plain program's by a relative error of at most 0.024.
Values may be sent and summed in bfloat16 or wider, within the bound.
No kernel may reach another device: no remote copies, remote signals or barrier semaphores. Data moves between devices by JAX's collectives and lax.ppermute only.
A program may use at most 128 MiB of HBM per device.

v0:
```python
import jax
import jax.numpy as jnp
from jax import lax
from jax.experimental import pallas as pl
from jax.experimental.pallas import tpu as pltpu
from jax.sharding import Mesh, PartitionSpec as P

HD = 64
TOK = 128
D = 768
HEADS = 3
WIDTH = HEADS * HD
CHUNK = 512
LOW = jnp.bfloat16
WIDE = jnp.float32


def dot(left, right, dims=((1,), (0,))):
    return lax.dot_general(left, right, (dims, ((), ())), preferred_element_type=WIDE)


def masked(scores, start, place, chunk, block):
    if chunk != block and chunk != 0 and block != 3:
        return scores
    spots = lax.broadcasted_iota(jnp.int32, scores.shape, 0) + chunk * CHUNK
    allowed = None
    if chunk == 0 or block == 3:
        allowed = spots >= start
    if chunk == block:
        causal = spots <= place
        allowed = causal if allowed is None else allowed & causal
    return jnp.where(allowed, scores, -1e30)


def chunk_rows(kv_ref, chunk, low, high):
    return jnp.concatenate(
        [kv_ref[y, chunk * TOK : (chunk + 1) * TOK, low:high] for y in range(4)], axis=0
    )


def forward_kernel(q_ref, kv_ref, bound_ref, att_ref, lse_ref):
    for block in range(4):
        rows = slice(block * TOK, (block + 1) * TOK)
        start = bound_ref[0:1, rows]
        place = bound_ref[1:2, rows]
        for head in range(HEADS):
            cols = slice(head * HD, (head + 1) * HD)
            query = q_ref[rows, cols]
            scores = []
            for chunk in range(block + 1):
                keys = chunk_rows(kv_ref, chunk, head * HD, head * HD + HD)
                scores.append(
                    masked(dot(keys, query, ((1,), (1,))), start, place, chunk, block)
                )
            top = scores[0].max(axis=0, keepdims=True)
            for item in scores[1:]:
                top = jnp.maximum(top, item.max(axis=0, keepdims=True))
            total = jnp.zeros((1, TOK), WIDE)
            summed = jnp.zeros((HD, TOK), WIDE)
            for chunk in range(block + 1):
                weights = jnp.exp(scores[chunk] - top)
                total = total + weights.sum(axis=0, keepdims=True)
                values = chunk_rows(kv_ref, chunk, WIDTH + head * HD, WIDTH + head * HD + HD)
                summed = summed + dot(values, weights.astype(LOW), ((0,), (0,)))
            att_ref[rows, cols] = jnp.transpose(summed / total).astype(LOW)
            lse_ref[head : head + 1, rows] = top + jnp.log(total)


def backward_kernel(q_ref, kv_ref, bound_ref, lse_ref, do_ref, dq_ref, dkv_ref, p_ref, ds_ref):
    for head in range(HEADS):
        cols = slice(head * HD, (head + 1) * HD)
        for block in range(4):
            rows = slice(block * TOK, (block + 1) * TOK)
            start = bound_ref[0:1, rows]
            place = bound_ref[1:2, rows]
            query = q_ref[rows, cols]
            d_out = do_ref[rows, cols]
            lse = lse_ref[head : head + 1, rows]
            delta = jnp.zeros((1, TOK), WIDE)
            probs, d_probs = [], []
            for chunk in range(block + 1):
                keys = chunk_rows(kv_ref, chunk, head * HD, head * HD + HD)
                scores = masked(dot(keys, query, ((1,), (1,))), start, place, chunk, block)
                prob = jnp.exp(scores - lse)
                values = chunk_rows(kv_ref, chunk, WIDTH + head * HD, WIDTH + head * HD + HD)
                d_prob = dot(values, d_out, ((1,), (1,)))
                delta = delta + (prob * d_prob).sum(axis=0, keepdims=True)
                p_ref[chunk * CHUNK : (chunk + 1) * CHUNK, rows] = prob.astype(LOW)
                probs.append(prob)
                d_probs.append(d_prob)
            d_query = jnp.zeros((HD, TOK), WIDE)
            for chunk in range(block + 1):
                d_score = (probs[chunk] * (d_probs[chunk] - delta)).astype(LOW)
                ds_ref[chunk * CHUNK : (chunk + 1) * CHUNK, rows] = d_score
                keys = chunk_rows(kv_ref, chunk, head * HD, head * HD + HD)
                d_query = d_query + dot(keys, d_score, ((0,), (0,)))
            dq_ref[rows, cols] = (jnp.transpose(d_query) * (HD**-0.5)).astype(LOW)
        for chunk in range(4):
            spots = slice(chunk * CHUNK, (chunk + 1) * CHUNK)
            later = slice(chunk * TOK, 4 * TOK)
            d_keys = dot(ds_ref[spots, later], q_ref[later, cols]).astype(LOW)
            d_values = dot(p_ref[spots, later], do_ref[later, cols]).astype(LOW)
            for y in range(4):
                part = slice(y * TOK, (y + 1) * TOK)
                place_rows = slice(chunk * TOK, (chunk + 1) * TOK)
                dkv_ref[y, place_rows, cols] = d_keys[part]
                dkv_ref[y, place_rows, WIDTH + head * HD : WIDTH + head * HD + HD] = d_values[part]


def ffn_kernel(
    own_ref,
    early_ref,
    att_ref,
    gathered_ref,
    up_ref,
    plain_ref,
    wide_ref,
    bias_ref,
    middle_ref,
    normed_hbm,
    act_hbm,
    d_up_hbm,
    d_normed_ref,
    out_hbm,
    sums_ref,
    mid_scr,
    up_scr,
    down_scr,
    cot_scr,
    normed_ref,
    act_ref,
    d_up_ref,
    out_ref,
    sems,
):
    copies = [
        pltpu.make_async_copy(source, target, sems.at[index])
        for index, (source, target) in enumerate(
            (
                (normed_ref, normed_hbm),
                (act_ref, act_hbm),
                (d_up_ref, d_up_hbm),
                (out_ref, out_hbm),
            )
        )
    ]
    for z in range(4):
        for y in range(4):
            row = (4 * z + y) * 48
            up_scr[row : row + 48] = up_ref[y, 48 * z : 48 * z + 48]
        down_scr[192 * z : 192 * z + 192] = plain_ref[z, 0:192]
        cot_scr[TOK * z : TOK * z + TOK] = gathered_ref[z, 0:TOK]
        mid_scr[TOK * z : TOK * z + TOK] = early_ref[z, 0:TOK].astype(WIDE)
    middle = mid_scr[...] + wide_ref[2:3, :]
    for z in range(4):
        middle = middle + dot(att_ref[z], gathered_ref[z, TOK : TOK + 192])
    mid_scr[...] = middle
    middle_ref[...] = mid_scr[pl.ds(pl.multiple_of(own_ref[0] * TOK, TOK), TOK), :]
    average = jnp.mean(middle, axis=-1, keepdims=True)
    centered = middle - average
    variance = jnp.mean(centered * centered, axis=-1, keepdims=True)
    hat = centered * lax.rsqrt(variance + 1e-05)
    normed = (hat * wide_ref[6:7, :] + wide_ref[7:8, :]).astype(LOW)
    normed_ref[...] = normed
    copies[0].start()
    upward = dot(normed, up_scr[...]) + bias_ref[...]
    root = 0.7978845608028654
    square = upward * upward
    bend = jnp.tanh(root * (upward + 0.044715 * (square * upward)))
    level = 0.5 * (1.0 + bend)
    activated = (upward * level).astype(LOW)
    act_ref[...] = activated
    copies[1].start()
    out_ref[...] = dot(activated, down_scr[...]).astype(LOW)
    copies[3].start()
    slope = level + 0.5 * upward * (1.0 - bend * bend) * (root * (1.0 + 0.134145 * square))
    d_act = dot(cot_scr[...], down_scr[...], ((1,), (1,)))
    d_upward = (d_act * slope).astype(LOW)
    d_up_ref[...] = d_upward
    copies[2].start()
    d_normed = dot(d_upward, up_scr[...], ((1,), (1,)))
    d_normed_ref[...] = d_normed.astype(LOW)
    sums_ref[0:1, :] = jnp.sum(d_normed * hat, axis=0, keepdims=True)
    sums_ref[1:2, :] = jnp.sum(d_normed, axis=0, keepdims=True)
    sums_ref[2:3, :] = jnp.sum(d_upward.astype(WIDE), axis=0, keepdims=True)
    sums_ref[3:8, :] = jnp.zeros((5, D), WIDE)
    for copy in copies:
        copy.wait()


def grad_kernel(normed_ref, d_up_ref, act_ref, gathered_ref, att_ref, branch_ref, out_ref, cot_scr):
    half = D // 2
    for z in range(4):
        cot_scr[TOK * z : TOK * z + TOK] = gathered_ref[z, 0:TOK]
    up = dot(normed_ref[...], d_up_ref[...], ((0,), (0,))).astype(LOW)
    down = dot(act_ref[...], cot_scr[...], ((0,), (0,))).astype(LOW)
    proj = dot(att_ref[...], branch_ref[...], ((0,), (0,))).astype(LOW)
    blank = jnp.zeros((16, half), LOW)
    for x in range(4):
        for core in range(2):
            cols = slice(core * half, core * half + half)
            slot = 2 * x + core
            for y in range(4):
                base = TOK * y
                for z in range(4):
                    row = (4 * z + y) * 48 + 16 * x
                    out_ref[slot, base + 16 * z : base + 16 * z + 16] = (
                        up[row : row + 16, cols] if x < 3 else blank
                    )
                row = 192 * y + 48 * x
                out_ref[slot, base + 64 : base + 112] = down[row : row + 48, cols]
                row = 48 * y + 16 * x
                out_ref[slot, base + 112 : base + 128] = (
                    proj[row : row + 16, cols] if x < 3 else blank
                )


def pack_kernel(
    tokens_hbm,
    qkv_hbm,
    up_hbm,
    down_hbm,
    proj_hbm,
    short_ref,
    hidden_ref,
    seg_ref,
    out_ref,
    plain_ref,
    tokens_ref,
    qkv_ref,
    up_ref,
    sems,
):
    pairs = (
        (tokens_hbm, tokens_ref),
        (qkv_hbm, qkv_ref),
        (up_hbm, up_ref),
        (down_hbm, plain_ref.at[pl.ds(0, 192)]),
        (proj_hbm, plain_ref.at[pl.ds(192, 48)]),
    )
    copies = [
        pltpu.make_async_copy(source, target, sems.at[index])
        for index, (source, target) in enumerate(pairs)
    ]
    for copy in copies:
        copy.start()
    seg = seg_ref[...]
    count_one = jnp.sum((seg <= 0).astype(WIDE), axis=1, keepdims=True)
    count_two = jnp.sum((seg <= 1).astype(WIDE), axis=1, keepdims=True)
    spot = lax.broadcasted_iota(jnp.int32, (1, 192), 1)
    counts = jnp.where(spot == 0, count_one, jnp.where(spot == 1, count_two, 0.0))
    side = jnp.concatenate(
        [
            jnp.concatenate(
                [short_ref[...].astype(WIDE), jnp.zeros((8, 144), WIDE)], axis=1
            ),
            jnp.concatenate(
                [hidden_ref[...].astype(WIDE), jnp.zeros((4, 144), WIDE)], axis=1
            ),
            counts,
            jnp.concatenate([seg.astype(WIDE), jnp.zeros((1, 64), WIDE)], axis=1),
            jnp.zeros((34, 192), WIDE),
        ],
        axis=0,
    ).astype(LOW)
    for copy in copies:
        copy.wait()
    for part in range(4):
        out_ref[part, 0:TOK, :] = tokens_ref[...]
        for kind in range(3):
            out_ref[part, TOK : TOK + 48, kind * WIDTH : (kind + 1) * WIDTH] = qkv_ref[
                :, kind * D + part * WIDTH : kind * D + (part + 1) * WIDTH
            ]
        out_ref[part, TOK : TOK + 48, 3 * WIDTH : D] = side
        out_ref[part, TOK + 48 : TOK + 96, :] = up_ref[:, part * D : (part + 1) * D]


def unpack_kernel(core_ref, mine_ref, theirs_ref, qkv_ref, out_ref, up_ref, down_ref, *line_refs):
    first = core_ref[0] == 0
    half = D // 2
    short = jnp.zeros((12, 48), WIDE)
    for part in range(4):
        mine = mine_ref[part].astype(WIDE)
        theirs = theirs_ref[part].astype(WIDE)
        sides = (jnp.where(first, mine, theirs), jnp.where(first, theirs, mine))
        rows = slice(16 * part, 16 * part + 16)
        for core in range(2):
            side = sides[core]
            cols = slice(core * half, (core + 1) * half)
            down_ref[part * 48 : (part + 1) * 48, cols] = side[TOK : TOK + 48]
            if part == 3:
                continue
            out_ref[rows, cols] = side[TOK + 48 : TOK + 64]
            for quarter in range(4):
                low = quarter * D + core * half
                up_ref[rows, low : low + half] = side[32 * quarter : 32 * quarter + 16]
                block = side[32 * quarter + 16 : 32 * quarter + 32]
                low = quarter * WIDTH
                if core == 0:
                    qkv_ref[rows, low : low + WIDTH] = block[:, :WIDTH]
                    qkv_ref[rows, D + low : D + low + WIDTH] = block[:, WIDTH:]
                else:
                    qkv_ref[rows, 2 * D + low : 2 * D + low + WIDTH] = block[:, :WIDTH]
                    if part == 0:
                        short = short + block[:12, WIDTH : WIDTH + 48]
    hidden = jnp.concatenate([short[2 + i : 3 + i] for i in range(4)], axis=1)
    lines = [short[i : i + 1] for i in (0, 1, 6)] + [hidden]
    lines += [short[i : i + 1] for i in range(7, 12)]
    for ref, value in zip(line_refs, lines):
        ref[...] = value


VMEM = pl.BlockSpec(memory_space=pltpu.VMEM)
FAR = pl.BlockSpec(memory_space=pltpu.HBM)
PARAMS = pltpu.CompilerParams(vmem_limit_bytes=48 * 1024 * 1024)
WHOLE = pltpu.CompilerParams(vmem_limit_bytes=60 * 1024 * 1024)


def attend_forward(query, kv, bounds):
    return pl.pallas_call(
        forward_kernel,
        out_shape=(
            jax.ShapeDtypeStruct((4 * TOK, WIDTH), LOW),
            jax.ShapeDtypeStruct((8, 4 * TOK), WIDE),
        ),
        in_specs=[VMEM] * 3,
        out_specs=(VMEM, VMEM),
        compiler_params=PARAMS,
        cost_estimate=pl.CostEstimate(
            flops=1_000_000_000, bytes_accessed=4_000_000, transcendentals=2_000_000
        ),
    )(query, kv, bounds)


def attend_backward(query, kv, bounds, lse, d_out):
    return pl.pallas_call(
        backward_kernel,
        out_shape=(
            jax.ShapeDtypeStruct((4 * TOK, WIDTH), LOW),
            jax.ShapeDtypeStruct((4, 4 * TOK, 2 * WIDTH), LOW),
        ),
        in_specs=[VMEM] * 5,
        out_specs=(VMEM, VMEM),
        scratch_shapes=[
            pltpu.VMEM((4 * CHUNK, 4 * TOK), LOW),
            pltpu.VMEM((4 * CHUNK, 4 * TOK), LOW),
        ],
        compiler_params=PARAMS,
        cost_estimate=pl.CostEstimate(
            flops=2_500_000_000, bytes_accessed=6_000_000, transcendentals=2_000_000
        ),
    )(query, kv, bounds, lse, d_out)


def feed_forward(*parts):
    return pl.pallas_call(
        ffn_kernel,
        out_shape=(
            jax.ShapeDtypeStruct((TOK, D), WIDE),
            jax.ShapeDtypeStruct((4 * TOK, D), LOW),
            jax.ShapeDtypeStruct((4 * TOK, D), LOW),
            jax.ShapeDtypeStruct((4 * TOK, D), LOW),
            jax.ShapeDtypeStruct((4 * TOK, D), LOW),
            jax.ShapeDtypeStruct((4 * TOK, D), LOW),
            jax.ShapeDtypeStruct((8, D), WIDE),
        ),
        in_specs=[pl.BlockSpec(memory_space=pltpu.SMEM)] + [VMEM] * 7,
        out_specs=(VMEM, FAR, FAR, FAR, VMEM, FAR, VMEM),
        scratch_shapes=[
            pltpu.VMEM((4 * TOK, D), WIDE),
            pltpu.VMEM((D, D), LOW),
            pltpu.VMEM((D, D), LOW),
            pltpu.VMEM((4 * TOK, D), LOW),
            pltpu.VMEM((4 * TOK, D), LOW),
            pltpu.VMEM((4 * TOK, D), LOW),
            pltpu.VMEM((4 * TOK, D), LOW),
            pltpu.VMEM((4 * TOK, D), LOW),
            pltpu.SemaphoreType.DMA((4,)),
        ],
        compiler_params=WHOLE,
        cost_estimate=pl.CostEstimate(
            flops=4_000_000_000, bytes_accessed=12_000_000, transcendentals=400_000
        ),
    )(*parts)


def weight_grads(*parts):
    return pl.pallas_call(
        grad_kernel,
        out_shape=jax.ShapeDtypeStruct((8, 4 * TOK, D // 2), LOW),
        in_specs=[VMEM] * 6,
        out_specs=VMEM,
        scratch_shapes=[pltpu.VMEM((4 * TOK, D), LOW)],
        compiler_params=PARAMS,
        cost_estimate=pl.CostEstimate(
            flops=1_400_000_000, bytes_accessed=9_000_000, transcendentals=0
        ),
    )(*parts)


def pack(*parts):
    return pl.pallas_call(
        pack_kernel,
        out_shape=(
            jax.ShapeDtypeStruct((4, TOK + 96, D), LOW),
            jax.ShapeDtypeStruct((240, D), LOW),
        ),
        in_specs=[FAR] * 5 + [VMEM] * 3,
        out_specs=(VMEM, VMEM),
        scratch_shapes=[
            pltpu.VMEM((TOK, D), LOW),
            pltpu.VMEM((48, 3 * D), LOW),
            pltpu.VMEM((48, 4 * D), LOW),
            pltpu.SemaphoreType.DMA((5,)),
        ],
        compiler_params=WHOLE,
        cost_estimate=pl.CostEstimate(
            flops=1_000_000, bytes_accessed=2_500_000, transcendentals=0
        ),
    )(*parts)


def unpack(core, mine, theirs):
    return pl.pallas_call(
        unpack_kernel,
        out_shape=tuple(
            jax.ShapeDtypeStruct(shape, WIDE)
            for shape in ((48, 3 * D), (48, D), (48, 4 * D), (192, D))
            + ((1, 48),) * 3
            + ((1, 192),)
            + ((1, 48),) * 5
        ),
        in_specs=[pl.BlockSpec(memory_space=pltpu.SMEM), VMEM, VMEM],
        out_specs=(VMEM,) * 13,
        compiler_params=PARAMS,
        cost_estimate=pl.CostEstimate(
            flops=1_000_000, bytes_accessed=3_500_000, transcendentals=0
        ),
    )(core, mine, theirs)


def norm_parts(values):
    average = jnp.mean(values, axis=-1, keepdims=True)
    centered = values - average
    variance = jnp.mean(centered * centered, axis=-1, keepdims=True)
    inverse = lax.rsqrt(variance + 1e-05)
    return centered * inverse, inverse


def norm_back(hat, inverse, gain, grad):
    scaled = grad * gain
    mean_one = jnp.mean(scaled, axis=-1, keepdims=True)
    mean_two = jnp.mean(scaled * hat, axis=-1, keepdims=True)
    return inverse * (scaled - mean_one - hat * mean_two)


def swap(value, axis):
    return lax.all_to_all(value, axis, 0, 0, tiled=True)


def share(value, axis):
    return swap(jnp.broadcast_to(value[None], (4,) + value.shape), axis)


def total(value):
    return jnp.sum(value.astype(WIDE), axis=0)


def other_core(value):
    return lax.ppermute(value, "c", [(0, 1), (1, 0)])


def body(
    tokens,
    segments,
    w_qkv,
    w_out,
    w_up,
    w_down,
    b_query,
    b_value,
    b_out,
    b_up,
    b_down,
    ln1_gain,
    ln1_shift,
    ln2_gain,
    ln2_shift,
    cotangent,
):
    ix, ic, iz, iy = (lax.axis_index(name) for name in ("x", "c", "z", "y"))
    first_doc = 3 * (2 * ix + ic)
    half = D // 2

    def lanes(value, core):
        return lax.dynamic_slice_in_dim(value, core * half, half, value.ndim - 1)

    short = jnp.stack(
        [b_query, b_value, b_out, b_down, ln1_gain, ln1_shift, ln2_gain, ln2_shift]
    )
    early, plain = pack(
        tokens,
        w_qkv,
        w_up,
        w_down,
        w_out,
        short,
        b_up.reshape(4, 48),
        (segments - first_doc)[None],
    )
    early = swap(early, "z")
    token_all = early[:, :TOK].reshape(4 * TOK, D)
    seg_all = early[:, TOK + 13, 576:704].astype(jnp.int32)
    early_all = share(early[:, TOK : TOK + 48, :640], "y").swapaxes(0, 1)
    qkv_part = early_all[:, :, :, :576].reshape(D, 3 * WIDTH)
    small_all = early_all[:, :, :16, 576:624].astype(WIDE)
    total_counts = jnp.sum(small_all[:, :, 12, :2], axis=(0, 1)).astype(jnp.int32)
    wide = small_all.reshape(16, 16, 48)[:, :8].swapaxes(0, 1).reshape(8, D)
    bias_out, bias_down, gain_one, shift_one, gain_two, shift_two = (
        wide[index] for index in range(2, 8)
    )
    own = lax.dynamic_index_in_dim(small_all, iz, 0, keepdims=False)
    bias_query = own[:, 0].reshape(WIDTH)
    bias_value = own[:, 1].reshape(WIDTH)
    bias_up = own[:, 8:12].reshape(D)

    plain = lax.all_gather(plain, "y")
    gathered = lax.all_gather(
        jnp.concatenate([cotangent, plain[:, 192:].reshape(192, D)], axis=0), "z"
    )
    up_rows, gathered = lax.optimization_barrier((early[:, TOK + 48 :], gathered))
    up_part = lax.all_gather(up_rows.reshape(192, D), "y")
    out_rows = lax.dynamic_index_in_dim(gathered, iz, 0, keepdims=False)[TOK:]
    cot_all = gathered[:, :TOK].reshape(4 * TOK, D)

    inputs = token_all.astype(WIDE)
    start = jnp.where(
        seg_all <= 0, 0, jnp.where(seg_all <= 1, total_counts[0], total_counts[1])
    )
    place = (
        4 * TOK * jnp.arange(4, dtype=jnp.int32)[:, None]
        + TOK * iy
        + jnp.arange(TOK, dtype=jnp.int32)[None, :]
    )
    bounds = jnp.concatenate(
        [start.reshape(1, 4 * TOK), place.reshape(1, 4 * TOK), jnp.zeros((6, 4 * TOK), jnp.int32)]
    )

    hat_one, inverse_one = norm_parts(inputs)
    normed_one = (hat_one * gain_one + shift_one).astype(LOW)
    qkv = dot(normed_one, qkv_part)
    query = ((qkv[:, :WIDTH] + bias_query).astype(LOW) * (HD**-0.5)).astype(LOW)
    kv = jnp.concatenate(
        [qkv[:, WIDTH : 2 * WIDTH], qkv[:, 2 * WIDTH :] + bias_value], axis=1
    ).astype(LOW)
    kv_all = share(kv, "y")
    att_part, lse = attend_forward(query, kv_all, bounds)
    att_all = share(att_part, "z")

    middle, normed_two, activated, d_upward, d_normed, out_part, sums = feed_forward(
        iz.astype(jnp.int32)[None], early, att_all, gathered, up_part, plain, wide, bias_up[None]
    )
    d_gain_two, d_shift_two, d_bias_up = sums[0], sums[1], sums[2]
    d_normed = total(swap(d_normed.reshape(4, TOK, D), "z"))
    own_rows = iz * TOK

    def mine(value):
        return lax.dynamic_slice_in_dim(value, own_rows, TOK, 0)

    hat_two, inverse_two = norm_parts(middle)
    d_middle = cotangent.astype(WIDE) + norm_back(hat_two, inverse_two, gain_two, d_normed)
    d_branch = d_middle.astype(LOW)
    branch_all = share(d_branch, "z").reshape(4 * TOK, D)
    d_attended = dot(branch_all, out_rows, ((1,), (1,))).astype(LOW)

    d_query, d_kv = attend_backward(query, kv_all, bounds, lse, d_attended)

    first = weight_grads(normed_two, d_upward, activated, gathered, att_part, branch_all)
    first = lax.psum_scatter(first, ("x", "c"), scatter_dimension=0, tiled=True)
    d_kv = total(swap(d_kv, "y")).astype(LOW)
    d_qkv = jnp.concatenate([d_query, d_kv], axis=1)
    d_normed = dot(d_qkv, qkv_part, ((1,), (1,)))
    d_gain_one = jnp.sum(d_normed * hat_one, axis=0)
    d_shift_one = jnp.sum(d_normed, axis=0)
    d_qkv_w = dot(normed_one, d_qkv, ((0,), (0,))).astype(LOW)

    d_qkv_sum = jnp.sum(d_qkv.astype(WIDE), axis=0)
    here = (jnp.arange(4) == iz).astype(WIDE)[:, None, None, None]
    of_z = jnp.concatenate(
        [
            d_qkv_sum[:WIDTH].reshape(4, 1, 48),
            d_qkv_sum[2 * WIDTH :].reshape(4, 1, 48),
            d_bias_up.reshape(4, 4, 48),
        ],
        axis=1,
    )
    of_all = jnp.stack(
        [
            jnp.sum(d_branch.astype(WIDE), axis=0),
            jnp.sum(cotangent.astype(WIDE), axis=0),
            d_gain_one,
            d_shift_one,
            d_gain_two,
            d_shift_two,
        ]
    )
    smalls = jnp.concatenate(
        [
            (of_z[None] * here).reshape(16, 6, 48),
            of_all.reshape(6, 16, 48).swapaxes(0, 1),
        ],
        axis=1,
    )
    smalls = jnp.pad(smalls.astype(LOW), ((0, 0), (0, 36), (0, 144)))
    second = jnp.concatenate([d_qkv_w.reshape(16, 48, 576), smalls], axis=2)
    got = other_core(lanes(second, 1 - ic))
    second = (lanes(second, ic).astype(WIDE) + got.astype(WIDE)).astype(LOW)
    second, late_normed = lax.optimization_barrier((second, d_normed))
    second = second.reshape(4, 4, 48, half).swapaxes(0, 1).reshape(4, 192, half)
    second = jnp.concatenate([first.reshape(4, TOK, half), second], axis=1)
    second = total(swap(second, "y")).astype(LOW)
    last = jnp.concatenate([late_normed.astype(LOW), out_part], axis=1).reshape(4, TOK, 2 * D)
    last = lax.psum_scatter(last, "z", scatter_dimension=0).astype(WIDE)
    d_normed = last[:, :D]
    out_tokens = (middle + last[:, D:] + bias_down).astype(LOW)
    d_tokens = (
        d_middle + norm_back(mine(hat_one), mine(inverse_one), gain_one, d_normed)
    ).astype(LOW)

    here_x = (jnp.arange(4) == ix)[:, None, None, None]
    spread = jnp.pad(second[TOK:].reshape(4, 48, half), ((0, 0), (0, 16), (0, 0)))
    joint = jnp.concatenate(
        [
            jnp.where(here_x, second[:64].reshape(1, 4, 16, half), jnp.zeros((), LOW)),
            spread.reshape(4, 4, 16, half).swapaxes(0, 1),
        ],
        axis=2,
    ).reshape(16, 32, half)
    joint = total(swap(joint, ("x", "z")).reshape(4, 4, 32, half)).astype(LOW)
    rows = second[64:TOK]
    whole = share(jnp.concatenate([joint.reshape(TOK, half), rows], axis=0), "x")
    theirs = other_core(whole)
    grads = unpack(ic.astype(jnp.int32)[None], whole, theirs)
    return (out_tokens, d_tokens) + grads[:4] + tuple(item[0] for item in grads[4:])


def solution(mesh):
    parts = Mesh(mesh.devices.reshape(4, 2, 4, 4), ("x", "c", "z", "y"))
    every = ("x", "c", "z", "y")
    group = ("z", "y")
    row, line = P(group, None), P(group)
    return jax.shard_map(
        body,
        mesh=parts,
        in_specs=(P(every, None), P(every)) + (row,) * 4 + (line,) * 9 + (P(every, None),),
        out_specs=(P(every, None),) * 2 + (row,) * 4 + (line,) * 9,
        check_vma=False,
    )
```

profile of v0, /device:TPU:1, one launch (start us, length us, event | category | flops | bytes accessed | tf_op | source)
XLA Modules:
  0.0 262.2 jit_solution(7456089430026300765)
XLA Ops:
  14.3 6.0 %all-to-all-start = ((bf16[4,224,768]{2,1,0:T(8,128)(2,1)}), bf16[4,224,768]{2,1,0:T(8,128)(2,1)S(1)}, u32[]{:S(2)}, u32[]{:S(2)}) async-start(bf16[4,224,768]{2,1,0:T(8,128)(2,1)} %get-tuple-element.45), calls=%async_computation | async-start | bytes 2752512 | tf_op jit(solution)/shard_map/all_to_all | solution.py:458
  20.3 23.0 %all-gather.8.cloned.1.call-done = bf16[960,768]{1,0:T(8,128)(2,1)} async-done(((bf16[240,768]{1,0:T(8,128)(2,1)}), bf16[960,768]{1,0:T(8,128)(2,1)}) %all-gather.8.cloned.1.call-update) | async-done | bytes 1474576 | tf_op jit(solution)/shard_map/all_gather | solution.py:527
  46.4 3.5 %all-to-all-start.1 = ((bf16[4,4,48,640]{3,2,1,0:T(8,128)(2,1)}), bf16[4,4,48,640]{3,2,1,0:T(8,128)(2,1)S(1)}, u32[]{:S(2)}, u32[]{:S(2)}) async-start(bf16[4,4,48,640]{3,2,1,0:T(8,128)(2,1)} %broadcast_in_dim.52), calls=%async_computation.1 | async-start | bytes 1966080 | tf_op jit(solution)/shard_map/all_to_all | solution.py:458
  51.6 12.0 %all-to-all-done.1 = bf16[4,4,48,640]{3,2,1,0:T(8,128)(2,1)S(1)} async-done(((bf16[4,4,48,640]{3,2,1,0:T(8,128)(2,1)}), bf16[4,4,48,640]{3,2,1,0:T(8,128)(2,1)S(1)}, u32[]{:S(2)}, u32[]{:S(2)}) %all-to-all-start.1) | async-done | bytes 983072 | tf_op jit(solution)/shard_map/all_to_all | solution.py:458
  68.9 3.6 %all-to-all-start.2 = ((bf16[4,512,384]{2,1,0:T(8,128)(2,1)}), bf16[4,512,384]{2,1,0:T(8,128)(2,1)S(1)}, u32[]{:S(2)}, u32[]{:S(2)}) async-start(bf16[4,512,384]{2,1,0:T(8,128)(2,1)} %broadcast_in_dim.53), calls=%async_computation.2 | async-start | bytes 3145728 | tf_op jit(solution)/shard_map/all_to_all | solution.py:458
  83.6 8.0 %all-to-all-done.2.kv_ref = bf16[4,512,384]{2,1,0:T(8,128)(2,1)S(1)} async-done(((bf16[4,512,384]{2,1,0:T(8,128)(2,1)}), bf16[4,512,384]{2,1,0:T(8,128)(2,1)S(1)}, u32[]{:S(2)}, u32[]{:S(2)}) %all-to-all-start.2) | async-done | bytes 1572896 | tf_op jit(solution)/shard_map/all_to_all | solution.py:458
  91.6 5.0 %shard_map.272 = (bf16[512,192]{1,0:T(8,128)(2,1)S(1)}, f32[8,512]{1,0:T(8,128)S(1)}) custom-call(bf16[512,192]{1,0:T(8,128)(2,1)S(1)} %fusion.15.q_ref, bf16[4,512,384]{2,1,0:T(8,128)(2,1)S(1)} %all-to-all-done.2.kv_ref, s32[8,512]{1,0:T(8,128)S(1)} %add_add_fusion.bound_ref), custom_call_target="tpu_custom_call" | custom-call | flops 1000000000 | bytes 4000000 | tf_op jit(solution)/shard_map/pallas_call | solution.py:320
  97.7 4.1 %all-to-all-start.3 = ((bf16[4,512,192]{1,2,0:T(8,128)(2,1)}), bf16[4,512,192]{1,2,0:T(8,128)(2,1)S(1)}, u32[]{:S(2)}, u32[]{:S(2)}) async-start(bf16[4,512,192]{1,2,0:T(8,128)(2,1)} %broadcast_in_dim.94), calls=%async_computation.3 | async-start | bytes 1572864 | tf_op jit(solution)/shard_map/all_to_all | solution.py:458
  103.9 6.2 %all-to-all-done.3 = bf16[4,512,192]{1,2,0:T(8,128)(2,1)S(1)} async-done(((bf16[4,512,192]{1,2,0:T(8,128)(2,1)}), bf16[4,512,192]{1,2,0:T(8,128)(2,1)S(1)}, u32[]{:S(2)}, u32[]{:S(2)}) %all-to-all-start.3) | async-done | bytes 786464 | tf_op jit(solution)/shard_map/all_to_all | solution.py:458
  111.4 9.0 %shard_map.273 = (f32[128,768]{1,0:T(8,128)}, bf16[512,768]{1,0:T(8,128)(2,1)}, bf16[512,768]{1,0:T(8,128)(2,1)}, bf16[512,768]{1,0:T(8,128)(2,1)}, bf16[512,768...) custom-call(s32[1]{0:T(128)} %bitcast.own_ref, bf16[4,224,768]{2,1,0:T(8,128)(2,1)} %copy-done.6, ...), custom_call_target="tpu_custom_call" | custom-call | flops 4000000000 | bytes 12000000 | tf_op jit(solution)/shard_map/pallas_call | solution.py:356
  120.5 3.6 %all-to-all-start.4 = ((bf16[4,128,768]{2,1,0:T(8,128)(2,1)}), bf16[4,128,768]{2,1,0:T(8,128)(2,1)S(1)}, u32[]{:S(2)}, u32[]{:S(2)}) async-start(bf16[4,128,768]{2,1,0:T(8,128)(2,1)} %bitcast.103), calls=%async_computation.4 | async-start | bytes 1572864 | tf_op jit(solution)/shard_map/all_to_all | solution.py:458
  124.6 7.8 %all-to-all-done.4 = bf16[4,128,768]{2,1,0:T(8,128)(2,1)S(1)} async-done(((bf16[4,128,768]{2,1,0:T(8,128)(2,1)}), bf16[4,128,768]{2,1,0:T(8,128)(2,1)S(1)}, u32[]{:S(2)}, u32[]{:S(2)}) %all-to-all-start.4) | async-done | bytes 786464 | tf_op jit(solution)/shard_map/all_to_all | solution.py:458
  133.8 10.9 %all_to_all.50 = bf16[4,128,768]{2,1,0:T(8,128)(2,1)S(1)} all-to-all(bf16[4,128,768]{2,1,0:T(8,128)(2,1)S(1)} %broadcast_in_dim.95), channel_id=1, replica_groups=mesh['x'=4,'c'=2,'z'=4,'y'=4] {'z'}, dimensions={0} | all-to-all | bytes 1572864 | tf_op jit(solution)/shard_map/all_to_all | solution.py:458
  150.0 9.8 %shard_map.274 = (bf16[512,192]{1,0:T(8,128)(2,1)S(1)}, bf16[4,512,384]{2,1,0:T(8,128)(2,1)}) custom-call(bf16[512,192]{1,0:T(8,128)(2,1)S(1)} %fusion.15.q_ref, bf16[4,512,384]{2,1,0:T(8,128)(2,1)S(1)} %copy-done.2, s32[8,512]{1,0:T(8,128)S(1)} %add_add_fusion.bound_ref, f32[8,512]{1,0:T(8,128)S(1)} %get-tuple-element.51.lse_ref, ...), custom_call_target="tpu_custom_call" | custom-call | flops 2500000000 | bytes 6000000 | tf_op jit(solution)/shard_map/pallas_call | solution.py:336
  159.7 3.6 %all-to-all-start.6 = ((bf16[4,512,384]{2,1,0:T(8,128)(2,1)}), bf16[4,512,384]{2,1,0:T(8,128)(2,1)S(1)}, u32[]{:S(2)}, u32[]{:S(2)}) async-start(bf16[4,512,384]{2,1,0:T(8,128)(2,1)} %get-tuple-element.54), calls=%async_computation.6 | async-start | bytes 3145728 | tf_op jit(solution)/shard_map/all_to_all | solution.py:458
  167.6 8.3 %all-to-all-done.6 = bf16[4,512,384]{2,1,0:T(8,128)(2,1)S(1)} async-done(((bf16[4,512,384]{2,1,0:T(8,128)(2,1)}), bf16[4,512,384]{2,1,0:T(8,128)(2,1)S(1)}, u32[]{:S(2)}, u32[]{:S(2)}) %all-to-all-start.6) | async-done | bytes 1572896 | tf_op jit(solution)/shard_map/all_to_all | solution.py:458
  180.5 3.6 %fusion.25 = (bf16[768]{0:T(1024)(128)(2,1)S(1)}, bf16[768]{0:T(1024)(128)(2,1)S(1)}, f32[512,768]{1,0:T(8,128)}, bf16[512,768]{1,0:T(8,128)(2,1)}) fusion(f32[512]{0:T(512)} %get-tuple-element.102, f32[512]{0:T(512)S(1)} %copy-done.25, bf16[4,224,768]{2,1,0:T(8,128)(2,1)S(1)} %copy-done.7, bf16[768,576]{1,0:T(8,128)(2,1)} %bitcast.96, ...), kind=kOutput, calls=%fused_computation.96 | convolution fusion | flops 456915456 | bytes 4627456 | tf_op jit(solution)/shard_map/dot_general | solution.py:19
  187.9 10.3 %collective-permute-start = (bf16[16,48,384]{2,1,0:T(8,128)(2,1)S(1)}, bf16[16,48,384]{2,1,0:T(8,128)(2,1)}, u32[]{:S(2)}, u32[]{:S(2)}) collective-permute-start(bf16[16,48,384]{2,1,0:T(8,128)(2,1)S(1)} %fusion.8), channel_id=1, source_target_pairs={{0,16},{16,0},{1,17},{17,1},{2,18},{18,2},{3,19},{19,3},{4,20},{20... | collective-permute-start | bytes 1769480 | tf_op jit(solution)/shard_map/ppermute | solution.py:470
  208.6 14.1 %all-to-all-done.7 = bf16[4,320,384]{2,1,0:T(8,128)(2,1)S(1)} async-done(((bf16[4,320,384]{2,1,0:T(8,128)(2,1)}), bf16[4,320,384]{2,1,0:T(8,128)(2,1)S(1)}, u32[]{:S(2)}, u32[]{:S(2)}) %all-to-all-start.7) | async-done | bytes 983072 | tf_op jit(solution)/shard_map/all_to_all | solution.py:458
  223.9 4.7 %all-to-all-start.8 = ((bf16[16,32,384]{2,1,0:T(8,128)(2,1)}), bf16[16,32,384]{2,1,0:T(8,128)(2,1)S(1)}, u32[]{:S(2)}, u32[]{:S(2)}) async-start(bf16[16,32,384]{2,1,0:T(8,128)(2,1)} %bitcast.47), calls=%async_computation.10 | async-start | bytes 786432 | tf_op jit(solution)/shard_map/all_to_all | solution.py:458
  229.3 7.4 %all-to-all-done.8 = bf16[16,32,384]{2,1,0:T(8,128)(2,1)S(1)} async-done(((bf16[16,32,384]{2,1,0:T(8,128)(2,1)}), bf16[16,32,384]{2,1,0:T(8,128)(2,1)S(1)}, u32[]{:S(2)}, u32[]{:S(2)}) %all-to-all-start.8) | async-done | bytes 393248 | tf_op jit(solution)/shard_map/all_to_all | solution.py:458
  237.7 3.6 %all-to-all-start.9 = ((bf16[4,192,384]{2,1,0:T(8,128)(2,1)}), bf16[4,192,384]{2,1,0:T(8,128)(2,1)S(1)}, u32[]{:S(2)}, u32[]{:S(2)}) async-start(bf16[4,192,384]{2,1,0:T(8,128)(2,1)} %broadcast_in_dim.101), calls=%async_computation.11 | async-start | bytes 1179648 | tf_op jit(solution)/shard_map/all_to_all | solution.py:458
  243.5 5.0 %all-to-all-done.9.mine_ref = bf16[4,192,384]{2,1,0:T(8,128)(2,1)S(1)} async-done(((bf16[4,192,384]{2,1,0:T(8,128)(2,1)}), bf16[4,192,384]{2,1,0:T(8,128)(2,1)S(1)}, u32[]{:S(2)}, u32[]{:S(2)}) %all-to-all-start.9) | async-done | bytes 589856 | tf_op jit(solution)/shard_map/all_to_all | solution.py:458
  248.6 3.8 %collective-permute-start.1 = (bf16[4,192,384]{2,1,0:T(8,128)(2,1)S(1)}, bf16[4,192,384]{2,1,0:T(8,128)(2,1)S(1)}, u32[]{:S(2)}, u32[]{:S(2)}) collective-permute-start(bf16[4,192,384]{2,1,0:T(8,128)(2,1)S(1)} %all-to-all-done.9.mine_ref), channel_id=1, source_target_pairs={{0,16},{16,0},{1,17},{17,1},{2,18},{18,2},{3,19},{19,3},{4,20},{20... | collective-permute-start | bytes 1769480 | tf_op jit(solution)/shard_map/ppermute | solution.py:470
  (180 shorter events, 70.7 us)
Async XLA Ops:
  7.2 36.2 %all-gather.8.cloned.1.call-start = ((), (), s32[]{:S(2)}) async-start(), calls=%async_computation.15 | async-start | bytes 1843200 | tf_op jit(solution)/shard_map/all_gather | solution.py:527
  14.3 30.0 %copy-start.15 = (bf16[128,768]{1,0:T(8,128)(2,1)S(1)}, bf16[128,768]{1,0:T(8,128)(2,1)}, u32[]{:S(2)}) copy-start(bf16[128,768]{1,0:T(8,128)(2,1)} %param.31) | copy-start | bytes 589828
  14.3 30.9 %all-to-all-start = ((bf16[4,224,768]{2,1,0:T(8,128)(2,1)}), bf16[4,224,768]{2,1,0:T(8,128)(2,1)S(1)}, u32[]{:S(2)}, u32[]{:S(2)}) async-start(bf16[4,224,768]{2,1,0:T(8,128)(2,1)} %get-tuple-element.45), calls=%async_computation | async-start | bytes 2752512 | tf_op jit(solution)/shard_map/all_to_all | solution.py:458
  20.3 55.7 %all-gather.10.cloned.1.call-start = ((), (), s32[]{:S(2)}) async-start(), calls=%async_computation.16 | async-start | bytes 2457600 | tf_op jit(solution)/shard_map/all_gather | solution.py:528
  45.2 35.5 %copy-start.6 = (bf16[4,224,768]{2,1,0:T(8,128)(2,1)}, bf16[4,224,768]{2,1,0:T(8,128)(2,1)S(1)}, u32[]{:S(2)}) copy-start(bf16[4,224,768]{2,1,0:T(8,128)(2,1)S(1)} %all-to-all-done.early_ref) | copy-start | bytes 4128772
  46.4 17.2 %all-to-all-start.1 = ((bf16[4,4,48,640]{3,2,1,0:T(8,128)(2,1)}), bf16[4,4,48,640]{3,2,1,0:T(8,128)(2,1)S(1)}, u32[]{:S(2)}, u32[]{:S(2)}) async-start(bf16[4,4,48,640]{3,2,1,0:T(8,128)(2,1)} %broadcast_in_dim.52), calls=%async_computation.1 | async-start | bytes 1966080 | tf_op jit(solution)/shard_map/all_to_all | solution.py:458
  51.6 14.3 %copy-start.21 = (f32[4,128]{1,0:T(4,128)}, f32[4,128]{1,0:T(4,128)S(1)}, u32[]{:S(2)}) copy-start(f32[4,128]{1,0:T(4,128)S(1)} %get-tuple-element.103) | copy-start | bytes 6148
  68.9 22.7 %all-to-all-start.2 = ((bf16[4,512,384]{2,1,0:T(8,128)(2,1)}), bf16[4,512,384]{2,1,0:T(8,128)(2,1)S(1)}, u32[]{:S(2)}, u32[]{:S(2)}) async-start(bf16[4,512,384]{2,1,0:T(8,128)(2,1)} %broadcast_in_dim.53), calls=%async_computation.2 | async-start | bytes 3145728 | tf_op jit(solution)/shard_map/all_to_all | solution.py:458
  72.5 38.9 %all-gather.6.cloned.1.call-start = ((), (), s32[]{:S(2)}) async-start(), calls=%async_computation.12 | async-start | bytes 1474560 | tf_op jit(solution)/shard_map/all_gather | solution.py:532
  97.7 12.5 %all-to-all-start.3 = ((bf16[4,512,192]{1,2,0:T(8,128)(2,1)}), bf16[4,512,192]{1,2,0:T(8,128)(2,1)S(1)}, u32[]{:S(2)}, u32[]{:S(2)}) async-start(bf16[4,512,192]{1,2,0:T(8,128)(2,1)} %broadcast_in_dim.94), calls=%async_computation.3 | async-start | bytes 1572864 | tf_op jit(solution)/shard_map/all_to_all | solution.py:458
  120.5 11.9 %all-to-all-start.4 = ((bf16[4,128,768]{2,1,0:T(8,128)(2,1)}), bf16[4,128,768]{2,1,0:T(8,128)(2,1)S(1)}, u32[]{:S(2)}, u32[]{:S(2)}) async-start(bf16[4,128,768]{2,1,0:T(8,128)(2,1)} %bitcast.103), calls=%async_computation.4 | async-start | bytes 1572864 | tf_op jit(solution)/shard_map/all_to_all | solution.py:458
  124.1 78.8 %reduce-scatter.5.cloned.1.call-start = ((), (), s32[]{:S(2)}) async-start(), calls=%async_computation.14 | async-start | bytes 3538944 | tf_op jit(solution)/shard_map/reduce_scatter | solution.py:579
  159.7 16.1 %all-to-all-start.6 = ((bf16[4,512,384]{2,1,0:T(8,128)(2,1)}), bf16[4,512,384]{2,1,0:T(8,128)(2,1)S(1)}, u32[]{:S(2)}, u32[]{:S(2)}) async-start(bf16[4,512,384]{2,1,0:T(8,128)(2,1)} %get-tuple-element.54), calls=%async_computation.6 | async-start | bytes 3145728 | tf_op jit(solution)/shard_map/all_to_all | solution.py:458
  163.3 78.0 %reduce-scatter.3.cloned.1.call-start = ((), (), s32[]{:S(2)}) async-start(), calls=%async_computation.13 | async-start | bytes 1966080 | tf_op jit(solution)/shard_map/reduce_scatter | solution.py:623
  167.6 13.0 %copy-start.25 = (f32[512]{0:T(512)S(1)}, f32[512]{0:T(512)}, u32[]{:S(2)}) copy-start(f32[512]{0:T(512)} %get-tuple-element.100) | copy-start | bytes 6148
  187.9 13.7 %copy-start.13 = (bf16[512,768]{1,0:T(8,128)(2,1)S(1)}, bf16[512,768]{1,0:T(8,128)(2,1)}, u32[]{:S(2)}) copy-start(bf16[512,768]{1,0:T(8,128)(2,1)} %get-tuple-element.57) | copy-start | bytes 2359300
  187.9 13.7 %copy-start.14 = (bf16[512,768]{1,0:T(8,128)(2,1)S(1)}, bf16[512,768]{1,0:T(8,128)(2,1)}, u32[]{:S(2)}) copy-start(bf16[512,768]{1,0:T(8,128)(2,1)} %get-tuple-element.56) | copy-start | bytes 2359300
  187.9 12.0 %collective-permute-start = (bf16[16,48,384]{2,1,0:T(8,128)(2,1)S(1)}, bf16[16,48,384]{2,1,0:T(8,128)(2,1)}, u32[]{:S(2)}, u32[]{:S(2)}) collective-permute-start(bf16[16,48,384]{2,1,0:T(8,128)(2,1)S(1)} %fusion.8), channel_id=1, source_target_pairs={{0,16},{16,0},{1,17},{17,1},{2,18},{18,2},{3,19},{19,3},{4,20},{20... | collective-permute-start | bytes 1769480 | tf_op jit(solution)/shard_map/ppermute | solution.py:470
  205.0 17.6 %all-to-all-start.7 = ((bf16[4,320,384]{2,1,0:T(8,128)(2,1)}), bf16[4,320,384]{2,1,0:T(8,128)(2,1)S(1)}, u32[]{:S(2)}, u32[]{:S(2)}) async-start(bf16[4,320,384]{2,1,0:T(8,128)(2,1)} %pad_maximum_fusion.1), calls=%async_computation.9 | async-start | bytes 1966080 | tf_op jit(solution)/shard_map/all_to_all | solution.py:458
  223.9 12.8 %all-to-all-start.8 = ((bf16[16,32,384]{2,1,0:T(8,128)(2,1)}), bf16[16,32,384]{2,1,0:T(8,128)(2,1)S(1)}, u32[]{:S(2)}, u32[]{:S(2)}) async-start(bf16[16,32,384]{2,1,0:T(8,128)(2,1)} %bitcast.47), calls=%async_computation.10 | async-start | bytes 786432 | tf_op jit(solution)/shard_map/all_to_all | solution.py:458
  237.7 14.7 %copy-start.9 = (f32[128,768]{1,0:T(8,128)S(1)}, f32[128,768]{1,0:T(8,128)}, u32[]{:S(2)}) copy-start(f32[128,768]{1,0:T(8,128)} %get-tuple-element.50) | copy-start | bytes 1179652
  237.7 14.7 %copy-start.11 = (f32[128,768]{1,0:T(8,128)S(1)}, f32[128,768]{1,0:T(8,128)}, u32[]{:S(2)}) copy-start(f32[128,768]{1,0:T(8,128)} %get-tuple-element.89) | copy-start | bytes 1179652
  237.7 10.9 %all-to-all-start.9 = ((bf16[4,192,384]{2,1,0:T(8,128)(2,1)}), bf16[4,192,384]{2,1,0:T(8,128)(2,1)S(1)}, u32[]{:S(2)}, u32[]{:S(2)}) async-start(bf16[4,192,384]{2,1,0:T(8,128)(2,1)} %broadcast_in_dim.101), calls=%async_computation.11 | async-start | bytes 1179648 | tf_op jit(solution)/shard_map/all_to_all | solution.py:458
  248.6 5.7 %collective-permute-start.1 = (bf16[4,192,384]{2,1,0:T(8,128)(2,1)S(1)}, bf16[4,192,384]{2,1,0:T(8,128)(2,1)S(1)}, u32[]{:S(2)}, u32[]{:S(2)}) collective-permute-start(bf16[4,192,384]{2,1,0:T(8,128)(2,1)S(1)} %all-to-all-done.9.mine_ref), channel_id=1, source_target_pairs={{0,16},{16,0},{1,17},{17,1},{2,18},{18,2},{3,19},{19,3},{4,20},{20... | collective-permute-start | bytes 1769480 | tf_op jit(solution)/shard_map/ppermute | solution.py:470
  (18 other events, 99.1 us)
Sparse Core Ops, SparseCore 0:
  14.4 28.8 all-gather.7
  45.6 30.4 all-gather.9
  78.3 24.7 all-gather.5
  148.1 38.4 reduce-scatter.4
  203.0 22.2 reduce-scatter.2
where the time goes:
time: 264 us; the launch traced here: 262 us
  waiting for transfers between devices  96 us (36%)
  starting transfers between devices  50.7 us (19%)
  Pallas kernels  31.6 us (12%)
  local copies, waits for them, and re-layouts  28.5 us (11%)
  other arithmetic  23.1 us (9%)
  between operations  14.5 us (5%)
  blocking collectives  10.9 us (4%)
  matrix products  6.81 us (3%)
    all_to_all x9, waiting for transfers between devices, swap(): return lax.all_to_all(value, axis, 0, 0, tiled=True)  68.9 us
    all_to_all x9, starting transfers between devices, swap(): return lax.all_to_all(value, axis, 0, 0, tiled=True)  36.2 us
    all_gather x1, waiting for transfers between devices, body(): plain = lax.all_gather(plain, 'y')  23 us
    ppermute x2, starting transfers between devices, other_core(): return lax.ppermute(value, 'c', [(0, 1), (1, 0)])  14.1 us
    all_to_all x1, blocking collectives, swap(): return lax.all_to_all(value, axis, 0, 0, tiled=True)  10.9 us
    pallas_call x1, Pallas kernels, attend_backward(): pl.pallas_call(backward_kernel, out_shape=(jax.ShapeDtypeStruct((4 * TOK,...  9.76 us
    pallas_call x1, Pallas kernels, feed_forward(): pl.pallas_call(ffn_kernel, out_shape=(jax.ShapeDtypeStruct((TOK, D), WIDE...  9.03 us
    dot_general x4, matrix products, dot(): lax.dot_general(left, right, (dims, ((), ())), preferred_element_type=WIDE)  6.81 us
  transfers between devices with their start and end apart: 16, of which 11 were waited for; matrix products, arithmetic and copies ran while one was open for 20% of the time, Pallas kernels for 6%

commit v1 on v0

--- a/solution.py
+++ b/solution.py
@@ -215,6 +215,66 @@
                 )
 
 
+def tail_kernel(
+    own_ref,
+    moved_ref,
+    query_ref,
+    weight_ref,
+    normed_ref,
+    early_ref,
+    sums_ref,
+    branch_ref,
+    cot_ref,
+    d_normed_ref,
+    out_ref,
+    hat_scr,
+):
+    half = D // 2
+    for z in range(4):
+        hat_scr[TOK * z : TOK * z + TOK] = early_ref[z, 0:TOK].astype(WIDE)
+    inputs = hat_scr[...]
+    centered = inputs - jnp.mean(inputs, axis=-1, keepdims=True)
+    variance = jnp.mean(centered * centered, axis=-1, keepdims=True)
+    hat = centered * lax.rsqrt(variance + 1e-05)
+    d_kv = moved_ref[0].astype(WIDE)
+    for y in range(1, 4):
+        d_kv = d_kv + moved_ref[y].astype(WIDE)
+    d_qkv = jnp.concatenate([query_ref[...].astype(WIDE), d_kv], axis=1).astype(LOW)
+    d_normed = dot(d_qkv, weight_ref[...], ((1,), (1,)))
+    d_normed_ref[...] = d_normed.astype(LOW)
+    d_weight = dot(normed_ref[...], d_qkv, ((0,), (0,)))
+    columns = jnp.sum(d_qkv.astype(WIDE), axis=0, keepdims=True)
+    wide_rows = [
+        jnp.sum(branch_ref[...].astype(WIDE), axis=0, keepdims=True),
+        jnp.sum(cot_ref[...].astype(WIDE), axis=0, keepdims=True),
+        jnp.sum(d_normed * hat, axis=0, keepdims=True),
+        jnp.sum(d_normed, axis=0, keepdims=True),
+        sums_ref[0:1, :],
+        sums_ref[1:2, :],
+    ]
+    hidden = sums_ref[2:3, :]
+    for y in range(4):
+        low = 48 * y
+        own_rows = [
+            columns[:, low : low + 48],
+            columns[:, 2 * WIDTH + low : 2 * WIDTH + low + 48],
+        ] + [hidden[:, 192 * y + 48 * i : 192 * y + 48 * i + 48] for i in range(4)]
+        own_rows = jnp.concatenate(own_rows, axis=0)
+        for z in range(4):
+            low = 48 * (4 * z + y)
+            short = jnp.concatenate(
+                [jnp.where(own_ref[0] == z, own_rows, 0.0)]
+                + [item[:, low : low + 48] for item in wide_rows]
+                + [jnp.zeros((36, 48), WIDE)],
+                axis=0,
+            )
+            block = d_weight[low : low + 48]
+            out_ref[0, y, 48 * z : 48 * z + 48] = block[:, :half].astype(LOW)
+            out_ref[1, y, 48 * z : 48 * z + 48] = jnp.concatenate(
+                [block[:, half:], short, jnp.zeros((48, 144), WIDE)], axis=1
+            ).astype(LOW)
+
+
 def pack_kernel(
     tokens_hbm,
     qkv_hbm,
@@ -398,6 +458,23 @@
     )(*parts)
 
 
+def tail(*parts):
+    return pl.pallas_call(
+        tail_kernel,
+        out_shape=(
+            jax.ShapeDtypeStruct((4 * TOK, D), LOW),
+            jax.ShapeDtypeStruct((2, 4, 192, D // 2), LOW),
+        ),
+        in_specs=[pl.BlockSpec(memory_space=pltpu.SMEM)] + [VMEM] * 8,
+        out_specs=(VMEM, VMEM),
+        scratch_shapes=[pltpu.VMEM((4 * TOK, D), WIDE)],
+        compiler_params=PARAMS,
+        cost_estimate=pl.CostEstimate(
+            flops=1_000_000_000, bytes_accessed=7_000_000, transcendentals=0
+        ),
+    )(*parts)
+
+
 def pack(*parts):
     return pl.pallas_call(
         pack_kernel,
@@ -511,7 +588,9 @@
     early = swap(early, "z")
     token_all = early[:, :TOK].reshape(4 * TOK, D)
     seg_all = early[:, TOK + 13, 576:704].astype(jnp.int32)
-    early_all = share(early[:, TOK : TOK + 48, :640], "y").swapaxes(0, 1)
+    payload = early[:, TOK : TOK + 48, :640]
+    payload = jnp.broadcast_to(payload[None], (4,) + payload.shape)
+    early_all = swap(payload, "y").swapaxes(0, 1)
     qkv_part = early_all[:, :, :, :576].reshape(D, 3 * WIDTH)
     small_all = early_all[:, :, :16, 576:624].astype(WIDE)
     total_counts = jnp.sum(small_all[:, :, 12, :2], axis=(0, 1)).astype(jnp.int32)
@@ -525,6 +604,7 @@
     bias_up = own[:, 8:12].reshape(D)
 
     plain = lax.all_gather(plain, "y")
+    plain, _ = lax.optimization_barrier((plain, payload))
     gathered = lax.all_gather(
         jnp.concatenate([cotangent, plain[:, 192:].reshape(192, D)], axis=0), "z"
     )
@@ -560,7 +640,6 @@
     middle, normed_two, activated, d_upward, d_normed, out_part, sums = feed_forward(
         iz.astype(jnp.int32)[None], early, att_all, gathered, up_part, plain, wide, bias_up[None]
     )
-    d_gain_two, d_shift_two, d_bias_up = sums[0], sums[1], sums[2]
     d_normed = total(swap(d_normed.reshape(4, TOK, D), "z"))
     own_rows = iz * TOK
 
@@ -577,49 +656,25 @@
 
     first = weight_grads(normed_two, d_upward, activated, gathered, att_part, branch_all)
     first = lax.psum_scatter(first, ("x", "c"), scatter_dimension=0, tiled=True)
-    d_kv = total(swap(d_kv, "y")).astype(LOW)
-    d_qkv = jnp.concatenate([d_query, d_kv], axis=1)
-    d_normed = dot(d_qkv, qkv_part, ((1,), (1,)))
-    d_gain_one = jnp.sum(d_normed * hat_one, axis=0)
-    d_shift_one = jnp.sum(d_normed, axis=0)
-    d_qkv_w = dot(normed_one, d_qkv, ((0,), (0,))).astype(LOW)
-
-    d_qkv_sum = jnp.sum(d_qkv.astype(WIDE), axis=0)
-    here = (jnp.arange(4) == iz).astype(WIDE)[:, None, None, None]
-    of_z = jnp.concatenate(
-        [
-            d_qkv_sum[:WIDTH].reshape(4, 1, 48),
-            d_qkv_sum[2 * WIDTH :].reshape(4, 1, 48),
-            d_bias_up.reshape(4, 4, 48),
-        ],
-        axis=1,
-    )
-    of_all = jnp.stack(
-        [
-            jnp.sum(d_branch.astype(WIDE), axis=0),
-            jnp.sum(cotangent.astype(WIDE), axis=0),
-            d_gain_one,
-            d_shift_one,
-            d_gain_two,
-            d_shift_two,
-        ]
-    )
-    smalls = jnp.concatenate(
-        [
-            (of_z[None] * here).reshape(16, 6, 48),
-            of_all.reshape(6, 16, 48).swapaxes(0, 1),
-        ],
-        axis=1,
-    )
-    smalls = jnp.pad(smalls.astype(LOW), ((0, 0), (0, 36), (0, 144)))
-    second = jnp.concatenate([d_qkv_w.reshape(16, 48, 576), smalls], axis=2)
-    got = other_core(lanes(second, 1 - ic))
-    second = (lanes(second, ic).astype(WIDE) + got.astype(WIDE)).astype(LOW)
+    d_kv = swap(d_kv, "y")
+    d_normed, second = tail(
+        iz.astype(jnp.int32)[None],
+        d_kv,
+        d_query,
+        qkv_part,
+        normed_one,
+        early,
+        sums,
+        d_branch,
+        cotangent,
+    )
+    got = other_core(lax.dynamic_index_in_dim(second, 1 - ic, 0, keepdims=False))
+    second = lax.dynamic_index_in_dim(second, ic, 0, keepdims=False)
+    second = (second.astype(WIDE) + got.astype(WIDE)).astype(LOW)
     second, late_normed = lax.optimization_barrier((second, d_normed))
-    second = second.reshape(4, 4, 48, half).swapaxes(0, 1).reshape(4, 192, half)
     second = jnp.concatenate([first.reshape(4, TOK, half), second], axis=1)
     second = total(swap(second, "y")).astype(LOW)
-    last = jnp.concatenate([late_normed.astype(LOW), out_part], axis=1).reshape(4, TOK, 2 * D)
+    last = jnp.concatenate([late_normed, out_part], axis=1).reshape(4, TOK, 2 * D)
     last = lax.psum_scatter(last, "z", scatter_dimension=0).astype(WIDE)
     d_normed = last[:, :D]
     out_tokens = (middle + last[:, D:] + bias_down).astype(LOW)

time: 264 us -> 263 us (level)
  blocking collectives: 10.9 us -> 34.2 us
  waiting for transfers between devices: 96 us -> 85.5 us
  local copies, waits for them, and re-layouts: 28.5 us -> 22.9 us
  Pallas kernels: 31.6 us -> 36.5 us
  matrix products: 6.81 us -> 2.06 us
  starting transfers between devices: 50.7 us -> 46.4 us
  other arithmetic: 23.1 us -> 19.1 us
    all_to_all x1 -> x2, blocking collectives: 10.9 us -> 34.2 us  [swap(): return lax.all_to_all(value, axis, 0, 0, tiled=True)]
    all_gather x1, waiting for transfers between devices: 23 us -> 5.63 us  [body(): plain = lax.all_gather(plain, 'y')]
    all_to_all x9 -> x8, waiting for transfers between devices: 68.9 us -> 75.9 us  [swap(): return lax.all_to_all(value, axis, 0, 0, tiled=True)]
    dot_general x4 -> x2, matrix products: 6.81 us -> 2.06 us  [dot(): lax.dot_general(left, right, (dims, ((), ())), preferred_element_type=WIDE)]
    all_to_all x9 -> x8, starting transfers between devices: 36.2 us -> 31.9 us  [swap(): return lax.all_to_all(value, axis, 0, 0, tiled=True)]
    unnamed x53 -> x45, local copies, waits for them, and re-layouts: 2.72 us -> 6.22 us
    pallas_call x0 -> x1, Pallas kernels: none -> 3.25 us  [tail(): pl.pallas_call(tail_kernel, out_shape=(jax.ShapeDtypeStruct((4 * TOK, D),...]
  transfers between devices with their start and end apart: 16 -> 15, of which waited for: 11 -> 11; matrix products, arithmetic and copies ran while one was open for 20% -> 12% of each run, Pallas kernels for 6% -> 8%
where the time goes in v1:
time: 263 us; the launch traced here: 261 us
  waiting for transfers between devices  85.5 us (33%)
  starting transfers between devices  46.4 us (18%)
  Pallas kernels  36.5 us (14%)
  blocking collectives  34.2 us (13%)
  local copies, waits for them, and re-layouts  22.9 us (9%)
  other arithmetic  19.1 us (7%)
  between operations  14.4 us (5%)
    all_to_all x8, waiting for transfers between devices, swap(): return lax.all_to_all(value, axis, 0, 0, tiled=True)  75.9 us
    all_to_all x2, blocking collectives, swap(): return lax.all_to_all(value, axis, 0, 0, tiled=True)  34.2 us
    all_to_all x8, starting transfers between devices, swap(): return lax.all_to_all(value, axis, 0, 0, tiled=True)  31.9 us
    ppermute x2, starting transfers between devices, other_core(): return lax.ppermute(value, 'c', [(0, 1), (1, 0)])  14 us
    pallas_call x1, Pallas kernels, attend_backward(): pl.pallas_call(backward_kernel, out_shape=(jax.ShapeDtypeStruct((4 * TOK,...  9.97 us
    pallas_call x1, Pallas kernels, feed_forward(): pl.pallas_call(ffn_kernel, out_shape=(jax.ShapeDtypeStruct((TOK, D), WIDE...  9.01 us
    pallas_call x1, Pallas kernels, attend_forward(): pl.pallas_call(forward_kernel, out_shape=(jax.ShapeDtypeStruct((4 * TOK,...  6.4 us
    unnamed x45, local copies, waits for them, and re-layouts  6.22 us
  transfers between devices with their start and end apart: 15, of which 11 were waited for; matrix products, arithmetic and copies ran while one was open for 12% of the time, Pallas kernels for 8%

profile of v1, /device:TPU:1, one launch (start us, length us, event | category | flops | bytes accessed | tf_op | source)
XLA Modules:
  0.0 261.1 jit_solution(142823180439264598)
XLA Ops:
  14.4 23.3 %all_to_all.50.early_ref = bf16[4,224,768]{2,1,0:T(8,128)(2,1)S(1)} all-to-all(bf16[4,224,768]{2,1,0:T(8,128)(2,1)} %get-tuple-element.48), channel_id=1, replica_groups=mesh['x'=4,'c'=2,'z'=4,'y'=4] {'z'}, dimensions={0} | all-to-all | bytes 2752512 | tf_op jit(solution)/shard_map/all_to_all | solution.py:535
  37.7 5.6 %all-gather.8.cloned.1.call-done = bf16[960,768]{1,0:T(8,128)(2,1)} async-done(((bf16[240,768]{1,0:T(8,128)(2,1)}), bf16[960,768]{1,0:T(8,128)(2,1)}) %all-gather.8.cloned.1.call-update) | async-done | bytes 1474576 | tf_op jit(solution)/shard_map/all_gather | solution.py:606
  46.3 3.5 %all-to-all-start.1 = ((bf16[4,4,48,640]{3,2,1,0:T(8,128)(2,1)}), bf16[4,4,48,640]{3,2,1,0:T(8,128)(2,1)S(1)}, u32[]{:S(2)}, u32[]{:S(2)}) async-start(bf16[4,4,48,640]{3,2,1,0:T(8,128)(2,1)} %broadcast_in_dim.52), calls=%async_computation.1 | async-start | bytes 1966080 | tf_op jit(solution)/shard_map/all_to_all | solution.py:535
  51.8 11.7 %all-to-all-done.1 = bf16[4,4,48,640]{3,2,1,0:T(8,128)(2,1)S(1)} async-done(((bf16[4,4,48,640]{3,2,1,0:T(8,128)(2,1)}), bf16[4,4,48,640]{3,2,1,0:T(8,128)(2,1)S(1)}, u32[]{:S(2)}, u32[]{:S(2)}) %all-to-all-start.1) | async-done | bytes 983072 | tf_op jit(solution)/shard_map/all_to_all | solution.py:535
  69.3 4.4 %all-to-all-start.2 = ((bf16[4,512,384]{2,1,0:T(8,128)(2,1)}), bf16[4,512,384]{2,1,0:T(8,128)(2,1)}, u32[]{:S(2)}, u32[]{:S(2)}) async-start(bf16[4,512,384]{2,1,0:T(8,128)(2,1)} %broadcast_in_dim.53), calls=%async_computation.2 | async-start | bytes 3145728 | tf_op jit(solution)/shard_map/all_to_all | solution.py:535
  80.4 12.5 %all-to-all-done.2.kv_ref = bf16[4,512,384]{2,1,0:T(8,128)(2,1)} async-done(((bf16[4,512,384]{2,1,0:T(8,128)(2,1)}), bf16[4,512,384]{2,1,0:T(8,128)(2,1)}, u32[]{:S(2)}, u32[]{:S(2)}) %all-to-all-start.2) | async-done | bytes 1572896 | tf_op jit(solution)/shard_map/all_to_all | solution.py:535
  92.9 6.4 %shard_map.272 = (bf16[512,192]{1,0:T(8,128)(2,1)S(1)}, f32[8,512]{1,0:T(8,128)S(1)}) custom-call(bf16[512,192]{1,0:T(8,128)(2,1)S(1)} %fusion.6.q_ref, bf16[4,512,384]{2,1,0:T(8,128)(2,1)} %all-to-all-done.2.kv_ref, s32[8,512]{1,0:T(8,128)S(1)} %add_add_fusion.bound_ref), custom_call_target="tpu_custom_call" | custom-call | flops 1000000000 | bytes 4000000 | tf_op jit(solution)/shard_map/pallas_call | solution.py:380
  100.4 4.1 %all-to-all-start.3 = ((bf16[4,512,192]{1,2,0:T(8,128)(2,1)}), bf16[4,512,192]{1,2,0:T(8,128)(2,1)S(1)}, u32[]{:S(2)}, u32[]{:S(2)}) async-start(bf16[4,512,192]{1,2,0:T(8,128)(2,1)} %broadcast_in_dim.93), calls=%async_computation.3 | async-start | bytes 1572864 | tf_op jit(solution)/shard_map/all_to_all | solution.py:535
  106.6 6.2 %all-to-all-done.3 = bf16[4,512,192]{1,2,0:T(8,128)(2,1)S(1)} async-done(((bf16[4,512,192]{1,2,0:T(8,128)(2,1)}), bf16[4,512,192]{1,2,0:T(8,128)(2,1)S(1)}, u32[]{:S(2)}, u32[]{:S(2)}) %all-to-all-start.3) | async-done | bytes 786464 | tf_op jit(solution)/shard_map/all_to_all | solution.py:535
  114.2 9.0 %shard_map.273 = (f32[128,768]{1,0:T(8,128)}, bf16[512,768]{1,0:T(8,128)(2,1)}, bf16[512,768]{1,0:T(8,128)(2,1)}, bf16[512,768]{1,0:T(8,128)(2,1)}, bf16[512,768...) custom-call(s32[1]{0:T(128)} %bitcast.own_ref, bf16[4,224,768]{2,1,0:T(8,128)(2,1)} %copy-done, ...), custom_call_target="tpu_custom_call" | custom-call | flops 4000000000 | bytes 12000000 | tf_op jit(solution)/shard_map/pallas_call | solution.py:416
  123.2 3.6 %all-to-all-start.4 = ((bf16[4,128,768]{2,1,0:T(8,128)(2,1)}), bf16[4,128,768]{2,1,0:T(8,128)(2,1)S(1)}, u32[]{:S(2)}, u32[]{:S(2)}) async-start(bf16[4,128,768]{2,1,0:T(8,128)(2,1)} %bitcast.93), calls=%async_computation.4 | async-start | bytes 1572864 | tf_op jit(solution)/shard_map/all_to_all | solution.py:535
  127.3 7.8 %all-to-all-done.4 = bf16[4,128,768]{2,1,0:T(8,128)(2,1)S(1)} async-done(((bf16[4,128,768]{2,1,0:T(8,128)(2,1)}), bf16[4,128,768]{2,1,0:T(8,128)(2,1)S(1)}, u32[]{:S(2)}, u32[]{:S(2)}) %all-to-all-start.4) | async-done | bytes 786464 | tf_op jit(solution)/shard_map/all_to_all | solution.py:535
  136.5 10.9 %all_to_all.51 = bf16[4,128,768]{2,1,0:T(8,128)(2,1)S(1)} all-to-all(bf16[4,128,768]{2,1,0:T(8,128)(2,1)S(1)} %broadcast_in_dim.94), channel_id=1, replica_groups=mesh['x'=4,'c'=2,'z'=4,'y'=4] {'z'}, dimensions={0} | all-to-all | bytes 1572864 | tf_op jit(solution)/shard_map/all_to_all | solution.py:535
  152.3 10.0 %shard_map.274 = (bf16[512,192]{1,0:T(8,128)(2,1)S(1)}, bf16[4,512,384]{2,1,0:T(8,128)(2,1)S(1)}) custom-call(bf16[512,192]{1,0:T(8,128)(2,1)S(1)} %fusion.6.q_ref, bf16[4,512,384]{2,1,0:T(8,128)(2,1)} %all-to-all-done.2.kv_ref, s32[8,512]{1,0:T(8,128)S(1)} %add_add_fusion.bound_ref, f32[8,512]{1,0:T(8,128)S(1)} %get-tuple-element.55.lse_ref, ...), custom_call_target="tpu_custom_call" | custom-call | flops 2500000000 | bytes 6000000 | tf_op jit(solution)/shard_map/pallas_call | solution.py:396
  164.1 4.5 %all-to-all-start.6 = ((bf16[4,512,384]{2,1,0:T(8,128)(2,1)}), bf16[4,512,384]{2,1,0:T(8,128)(2,1)}, u32[]{:S(2)}, u32[]{:S(2)}) async-start(bf16[4,512,384]{2,1,0:T(8,128)(2,1)} %copy-done.4), calls=%async_computation.6 | async-start | bytes 3145728 | tf_op jit(solution)/shard_map/all_to_all | solution.py:535
  171.2 10.1 %all-to-all-done.6.moved_ref = bf16[4,512,384]{2,1,0:T(8,128)(2,1)} async-done(((bf16[4,512,384]{2,1,0:T(8,128)(2,1)}), bf16[4,512,384]{2,1,0:T(8,128)(2,1)}, u32[]{:S(2)}, u32[]{:S(2)}) %all-to-all-start.6) | async-done | bytes 1572896 | tf_op jit(solution)/shard_map/all_to_all | solution.py:535
  187.5 10.2 %collective-permute-start = (bf16[4,192,384]{2,1,0:T(8,128)(2,1)S(1)}, bf16[4,192,384]{2,1,0:T(8,128)(2,1)S(1)}, u32[]{:S(2)}, u32[]{:S(2)}) collective-permute-start(bf16[4,192,384]{2,1,0:T(8,128)(2,1)S(1)} %dynamic-slice_bitcast_fusion), channel_id=1, source_target_pairs={{0,16},{16,0},{1,17},{17,1},{2,18},{18,2},{3,19},{19,3},{4,20},{20... | collective-permute-start | bytes 1769480 | tf_op jit(solution)/shard_map/ppermute | solution.py:547
  204.0 3.5 %all-to-all-start.7 = ((bf16[4,320,384]{2,1,0:T(8,128)(2,1)}), bf16[4,320,384]{2,1,0:T(8,128)(2,1)S(1)}, u32[]{:S(2)}, u32[]{:S(2)}) async-start(bf16[4,320,384]{2,1,0:T(8,128)(2,1)} %pad_maximum_fusion.1), calls=%async_computation.9 | async-start | bytes 1966080 | tf_op jit(solution)/shard_map/all_to_all | solution.py:535
  207.5 14.1 %all-to-all-done.7 = bf16[4,320,384]{2,1,0:T(8,128)(2,1)S(1)} async-done(((bf16[4,320,384]{2,1,0:T(8,128)(2,1)}), bf16[4,320,384]{2,1,0:T(8,128)(2,1)S(1)}, u32[]{:S(2)}, u32[]{:S(2)}) %all-to-all-start.7) | async-done | bytes 983072 | tf_op jit(solution)/shard_map/all_to_all | solution.py:535
  222.8 4.7 %all-to-all-start.8 = ((bf16[16,32,384]{2,1,0:T(8,128)(2,1)}), bf16[16,32,384]{2,1,0:T(8,128)(2,1)S(1)}, u32[]{:S(2)}, u32[]{:S(2)}) async-start(bf16[16,32,384]{2,1,0:T(8,128)(2,1)} %bitcast.43), calls=%async_computation.10 | async-start | bytes 786432 | tf_op jit(solution)/shard_map/all_to_all | solution.py:535
  228.3 7.4 %all-to-all-done.8 = bf16[16,32,384]{2,1,0:T(8,128)(2,1)S(1)} async-done(((bf16[16,32,384]{2,1,0:T(8,128)(2,1)}), bf16[16,32,384]{2,1,0:T(8,128)(2,1)S(1)}, u32[]{:S(2)}, u32[]{:S(2)}) %all-to-all-start.8) | async-done | bytes 393248 | tf_op jit(solution)/shard_map/all_to_all | solution.py:535
  236.6 3.6 %all-to-all-start.9 = ((bf16[4,192,384]{2,1,0:T(8,128)(2,1)}), bf16[4,192,384]{2,1,0:T(8,128)(2,1)S(1)}, u32[]{:S(2)}, u32[]{:S(2)}) async-start(bf16[4,192,384]{2,1,0:T(8,128)(2,1)} %broadcast_in_dim.100), calls=%async_computation.11 | async-start | bytes 1179648 | tf_op jit(solution)/shard_map/all_to_all | solution.py:535
  241.5 6.0 %all-to-all-done.9.mine_ref = bf16[4,192,384]{2,1,0:T(8,128)(2,1)S(1)} async-done(((bf16[4,192,384]{2,1,0:T(8,128)(2,1)}), bf16[4,192,384]{2,1,0:T(8,128)(2,1)S(1)}, u32[]{:S(2)}, u32[]{:S(2)}) %all-to-all-start.9) | async-done | bytes 589856 | tf_op jit(solution)/shard_map/all_to_all | solution.py:535
  247.5 3.8 %collective-permute-start.1 = (bf16[4,192,384]{2,1,0:T(8,128)(2,1)S(1)}, bf16[4,192,384]{2,1,0:T(8,128)(2,1)S(1)}, u32[]{:S(2)}, u32[]{:S(2)}) collective-permute-start(bf16[4,192,384]{2,1,0:T(8,128)(2,1)S(1)} %all-to-all-done.9.mine_ref), channel_id=1, source_target_pairs={{0,16},{16,0},{1,17},{17,1},{2,18},{18,2},{3,19},{19,3},{4,20},{20... | collective-permute-start | bytes 1769480 | tf_op jit(solution)/shard_map/ppermute | solution.py:547
  (146 shorter events, 59.7 us)
Async XLA Ops:
  7.2 36.2 %all-gather.8.cloned.1.call-start = ((), (), s32[]{:S(2)}) async-start(), calls=%async_computation.15 | async-start | bytes 1843200 | tf_op jit(solution)/shard_map/all_gather | solution.py:606
  14.3 62.5 %all-gather.10.cloned.1.call-start = ((), (), s32[]{:S(2)}) async-start(), calls=%async_computation.16 | async-start | bytes 2457600 | tf_op jit(solution)/shard_map/all_gather | solution.py:608
  37.7 41.2 %copy-start = (bf16[4,224,768]{2,1,0:T(8,128)(2,1)}, bf16[4,224,768]{2,1,0:T(8,128)(2,1)S(1)}, u32[]{:S(2)}) copy-start(bf16[4,224,768]{2,1,0:T(8,128)(2,1)S(1)} %all_to_all.50.early_ref) | copy-start | bytes 4128772
  37.7 7.7 %copy-start.3 = (bf16[128,768]{1,0:T(8,128)(2,1)S(1)}, bf16[128,768]{1,0:T(8,128)(2,1)}, u32[]{:S(2)}) copy-start(bf16[128,768]{1,0:T(8,128)(2,1)} %cot_ref.1) | copy-start | bytes 589828
  46.3 17.2 %all-to-all-start.1 = ((bf16[4,4,48,640]{3,2,1,0:T(8,128)(2,1)}), bf16[4,4,48,640]{3,2,1,0:T(8,128)(2,1)S(1)}, u32[]{:S(2)}, u32[]{:S(2)}) async-start(bf16[4,4,48,640]{3,2,1,0:T(8,128)(2,1)} %broadcast_in_dim.52), calls=%async_computation.1 | async-start | bytes 1966080 | tf_op jit(solution)/shard_map/all_to_all | solution.py:535
  69.3 23.5 %all-to-all-start.2 = ((bf16[4,512,384]{2,1,0:T(8,128)(2,1)}), bf16[4,512,384]{2,1,0:T(8,128)(2,1)}, u32[]{:S(2)}, u32[]{:S(2)}) async-start(bf16[4,512,384]{2,1,0:T(8,128)(2,1)} %broadcast_in_dim.53), calls=%async_computation.2 | async-start | bytes 3145728 | tf_op jit(solution)/shard_map/all_to_all | solution.py:535
  73.7 40.5 %all-gather.6.cloned.1.call-start = ((), (), s32[]{:S(2)}) async-start(), calls=%async_computation.12 | async-start | bytes 1474560 | tf_op jit(solution)/shard_map/all_gather | solution.py:612
  100.4 12.5 %all-to-all-start.3 = ((bf16[4,512,192]{1,2,0:T(8,128)(2,1)}), bf16[4,512,192]{1,2,0:T(8,128)(2,1)S(1)}, u32[]{:S(2)}, u32[]{:S(2)}) async-start(bf16[4,512,192]{1,2,0:T(8,128)(2,1)} %broadcast_in_dim.93), calls=%async_computation.3 | async-start | bytes 1572864 | tf_op jit(solution)/shard_map/all_to_all | solution.py:535
  123.2 11.9 %all-to-all-start.4 = ((bf16[4,128,768]{2,1,0:T(8,128)(2,1)}), bf16[4,128,768]{2,1,0:T(8,128)(2,1)S(1)}, u32[]{:S(2)}, u32[]{:S(2)}) async-start(bf16[4,128,768]{2,1,0:T(8,128)(2,1)} %bitcast.93), calls=%async_computation.4 | async-start | bytes 1572864 | tf_op jit(solution)/shard_map/all_to_all | solution.py:535
  126.9 75.0 %reduce-scatter.5.cloned.1.call-start = ((), (), s32[]{:S(2)}) async-start(), calls=%async_computation.14 | async-start | bytes 3538944 | tf_op jit(solution)/shard_map/reduce_scatter | solution.py:658
  135.3 12.1 %copy-start.8 = (bf16[512,768]{1,0:T(8,128)(2,1)S(1)}, bf16[512,768]{1,0:T(8,128)(2,1)}, u32[]{:S(2)}) copy-start(bf16[512,768]{1,0:T(8,128)(2,1)} %get-tuple-element.65.d_up_ref) | copy-start | bytes 2359300
  135.5 11.9 %copy-start.6 = (bf16[512,768]{1,0:T(8,128)(2,1)S(1)}, bf16[512,768]{1,0:T(8,128)(2,1)}, u32[]{:S(2)}) copy-start(bf16[512,768]{1,0:T(8,128)(2,1)} %get-tuple-element.64.normed_ref) | copy-start | bytes 2359300
  135.5 11.9 %copy-start.7 = (bf16[512,768]{1,0:T(8,128)(2,1)S(1)}, bf16[512,768]{1,0:T(8,128)(2,1)}, u32[]{:S(2)}) copy-start(bf16[512,768]{1,0:T(8,128)(2,1)} %get-tuple-element.66.act_ref) | copy-start | bytes 2359300
  136.5 11.0 %copy-start.2 = (bf16[1280,768]{1,0:T(8,128)(2,1)S(1)}, bf16[1280,768]{1,0:T(8,128)(2,1)}, u32[]{:S(2)}) copy-start(bf16[1280,768]{1,0:T(8,128)(2,1)} %all-gather.10.cloned.1.call-done) | copy-start | bytes 5898244
  164.1 17.1 %all-to-all-start.6 = ((bf16[4,512,384]{2,1,0:T(8,128)(2,1)}), bf16[4,512,384]{2,1,0:T(8,128)(2,1)}, u32[]{:S(2)}, u32[]{:S(2)}) async-start(bf16[4,512,384]{2,1,0:T(8,128)(2,1)} %copy-done.4), calls=%async_computation.6 | async-start | bytes 3145728 | tf_op jit(solution)/shard_map/all_to_all | solution.py:535
  168.6 71.6 %reduce-scatter.3.cloned.1.call-start = ((), (), s32[]{:S(2)}) async-start(), calls=%async_computation.13 | async-start | bytes 1966080 | tf_op jit(solution)/shard_map/reduce_scatter | solution.py:678
  186.2 14.3 %copy-start.17 = (bf16[512,768]{1,0:T(8,128)(2,1)S(1)}, bf16[512,768]{1,0:T(8,128)(2,1)}, u32[]{:S(2)}) copy-start(bf16[512,768]{1,0:T(8,128)(2,1)} %get-tuple-element.63) | copy-start | bytes 2359300
  187.5 11.8 %collective-permute-start = (bf16[4,192,384]{2,1,0:T(8,128)(2,1)S(1)}, bf16[4,192,384]{2,1,0:T(8,128)(2,1)S(1)}, u32[]{:S(2)}, u32[]{:S(2)}) collective-permute-start(bf16[4,192,384]{2,1,0:T(8,128)(2,1)S(1)} %dynamic-slice_bitcast_fusion), channel_id=1, source_target_pairs={{0,16},{16,0},{1,17},{17,1},{2,18},{18,2},{3,19},{19,3},{4,20},{20... | collective-permute-start | bytes 1769480 | tf_op jit(solution)/shard_map/ppermute | solution.py:547
  204.0 17.6 %all-to-all-start.7 = ((bf16[4,320,384]{2,1,0:T(8,128)(2,1)}), bf16[4,320,384]{2,1,0:T(8,128)(2,1)S(1)}, u32[]{:S(2)}, u32[]{:S(2)}) async-start(bf16[4,320,384]{2,1,0:T(8,128)(2,1)} %pad_maximum_fusion.1), calls=%async_computation.9 | async-start | bytes 1966080 | tf_op jit(solution)/shard_map/all_to_all | solution.py:535
  222.8 12.8 %all-to-all-start.8 = ((bf16[16,32,384]{2,1,0:T(8,128)(2,1)}), bf16[16,32,384]{2,1,0:T(8,128)(2,1)S(1)}, u32[]{:S(2)}, u32[]{:S(2)}) async-start(bf16[16,32,384]{2,1,0:T(8,128)(2,1)} %bitcast.43), calls=%async_computation.10 | async-start | bytes 786432 | tf_op jit(solution)/shard_map/all_to_all | solution.py:535
  235.7 5.6 %copy-start.16 = (f32[512,768]{1,0:T(8,128)S(1)}, f32[512,768]{1,0:T(8,128)}, u32[]{:S(2)}) copy-start(f32[512,768]{1,0:T(8,128)} %get-tuple-element.93) | copy-start | bytes 4718596
  236.6 14.7 %copy-start.15 = (f32[128,768]{1,0:T(8,128)S(1)}, f32[128,768]{1,0:T(8,128)}, u32[]{:S(2)}) copy-start(f32[128,768]{1,0:T(8,128)} %get-tuple-element.54) | copy-start | bytes 1179652
  236.6 10.9 %all-to-all-start.9 = ((bf16[4,192,384]{2,1,0:T(8,128)(2,1)}), bf16[4,192,384]{2,1,0:T(8,128)(2,1)S(1)}, u32[]{:S(2)}, u32[]{:S(2)}) async-start(bf16[4,192,384]{2,1,0:T(8,128)(2,1)} %broadcast_in_dim.100), calls=%async_computation.11 | async-start | bytes 1179648 | tf_op jit(solution)/shard_map/all_to_all | solution.py:535
  247.5 5.7 %collective-permute-start.1 = (bf16[4,192,384]{2,1,0:T(8,128)(2,1)S(1)}, bf16[4,192,384]{2,1,0:T(8,128)(2,1)S(1)}, u32[]{:S(2)}, u32[]{:S(2)}) collective-permute-start(bf16[4,192,384]{2,1,0:T(8,128)(2,1)S(1)} %all-to-all-done.9.mine_ref), channel_id=1, source_target_pairs={{0,16},{16,0},{1,17},{17,1},{2,18},{18,2},{3,19},{19,3},{4,20},{20... | collective-permute-start | bytes 1769480 | tf_op jit(solution)/shard_map/ppermute | solution.py:547
  (13 other events, 28.5 us)
Sparse Core Ops, SparseCore 0:
  14.5 28.8 all-gather.7
  46.4 30.4 all-gather.9
  79.1 25.1 all-gather.5
  150.9 38.5 reduce-scatter.4
  202.0 22.2 reduce-scatter.2

commit v2 on v1

--- a/solution.py
+++ b/solution.py
@@ -62,7 +62,9 @@
                 total = total + weights.sum(axis=0, keepdims=True)
                 values = chunk_rows(kv_ref, chunk, WIDTH + head * HD, WIDTH + head * HD + HD)
                 summed = summed + dot(values, weights.astype(LOW), ((0,), (0,)))
-            att_ref[rows, cols] = jnp.transpose(summed / total).astype(LOW)
+            mixed = jnp.transpose(summed / total).astype(LOW)
+            for copy in range(4):
+                att_ref[copy, rows, cols] = mixed
             lse_ref[head : head + 1, rows] = top + jnp.log(total)
 
 
@@ -194,7 +196,7 @@
         cot_scr[TOK * z : TOK * z + TOK] = gathered_ref[z, 0:TOK]
     up = dot(normed_ref[...], d_up_ref[...], ((0,), (0,))).astype(LOW)
     down = dot(act_ref[...], cot_scr[...], ((0,), (0,))).astype(LOW)
-    proj = dot(att_ref[...], branch_ref[...], ((0,), (0,))).astype(LOW)
+    proj = dot(att_ref[0], branch_ref[...], ((0,), (0,))).astype(LOW)
     blank = jnp.zeros((16, half), LOW)
     for x in range(4):
         for core in range(2):
@@ -380,7 +382,7 @@
     return pl.pallas_call(
         forward_kernel,
         out_shape=(
-            jax.ShapeDtypeStruct((4 * TOK, WIDTH), LOW),
+            jax.ShapeDtypeStruct((4, 4 * TOK, WIDTH), LOW),
             jax.ShapeDtypeStruct((8, 4 * TOK), WIDE),
         ),
         in_specs=[VMEM] * 3,
@@ -603,8 +605,11 @@
     bias_value = own[:, 1].reshape(WIDTH)
     bias_up = own[:, 8:12].reshape(D)
 
+    inputs = token_all.astype(WIDE)
+    hat_one, inverse_one = norm_parts(inputs)
+
     plain = lax.all_gather(plain, "y")
-    plain, _ = lax.optimization_barrier((plain, payload))
+    plain, _ = lax.optimization_barrier((plain, inverse_one))
     gathered = lax.all_gather(
         jnp.concatenate([cotangent, plain[:, 192:].reshape(192, D)], axis=0), "z"
     )
@@ -613,7 +618,6 @@
     out_rows = lax.dynamic_index_in_dim(gathered, iz, 0, keepdims=False)[TOK:]
     cot_all = gathered[:, :TOK].reshape(4 * TOK, D)
 
-    inputs = token_all.astype(WIDE)
     start = jnp.where(
         seg_all <= 0, 0, jnp.where(seg_all <= 1, total_counts[0], total_counts[1])
     )
@@ -626,7 +630,6 @@
         [start.reshape(1, 4 * TOK), place.reshape(1, 4 * TOK), jnp.zeros((6, 4 * TOK), jnp.int32)]
     )
 
-    hat_one, inverse_one = norm_parts(inputs)
     normed_one = (hat_one * gain_one + shift_one).astype(LOW)
     qkv = dot(normed_one, qkv_part)
     query = ((qkv[:, :WIDTH] + bias_query).astype(LOW) * (HD**-0.5)).astype(LOW)
@@ -635,7 +638,7 @@
     ).astype(LOW)
     kv_all = share(kv, "y")
     att_part, lse = attend_forward(query, kv_all, bounds)
-    att_all = share(att_part, "z")
+    att_all = swap(att_part, "z")
 
     middle, normed_two, activated, d_upward, d_normed, out_part, sums = feed_forward(
         iz.astype(jnp.int32)[None], early, att_all, gathered, up_part, plain, wide, bias_up[None]
@@ -656,6 +659,8 @@
 
     first = weight_grads(normed_two, d_upward, activated, gathered, att_part, branch_all)
     first = lax.psum_scatter(first, ("x", "c"), scatter_dimension=0, tiled=True)
+    first = first.reshape(4 * TOK, half)
+    first = lax.psum_scatter(first, "y", scatter_dimension=0, tiled=True)
     d_kv = swap(d_kv, "y")
     d_normed, second = tail(
         iz.astype(jnp.int32)[None],
@@ -672,7 +677,6 @@
     second = lax.dynamic_index_in_dim(second, ic, 0, keepdims=False)
     second = (second.astype(WIDE) + got.astype(WIDE)).astype(LOW)
     second, late_normed = lax.optimization_barrier((second, d_normed))
-    second = jnp.concatenate([first.reshape(4, TOK, half), second], axis=1)
     second = total(swap(second, "y")).astype(LOW)
     last = jnp.concatenate([late_normed, out_part], axis=1).reshape(4, TOK, 2 * D)
     last = lax.psum_scatter(last, "z", scatter_dimension=0).astype(WIDE)
@@ -683,16 +687,16 @@
     ).astype(LOW)
 
     here_x = (jnp.arange(4) == ix)[:, None, None, None]
-    spread = jnp.pad(second[TOK:].reshape(4, 48, half), ((0, 0), (0, 16), (0, 0)))
+    spread = jnp.pad(second.reshape(4, 48, half), ((0, 0), (0, 16), (0, 0)))
     joint = jnp.concatenate(
         [
-            jnp.where(here_x, second[:64].reshape(1, 4, 16, half), jnp.zeros((), LOW)),
+            jnp.where(here_x, first[:64].reshape(1, 4, 16, half), jnp.zeros((), LOW)),
             spread.reshape(4, 4, 16, half).swapaxes(0, 1),
         ],
         axis=2,
     ).reshape(16, 32, half)
     joint = total(swap(joint, ("x", "z")).reshape(4, 4, 32, half)).astype(LOW)
-    rows = second[64:TOK]
+    rows = first[64:]
     whole = share(jnp.concatenate([joint.reshape(TOK, half), rows], axis=0), "x")
     theirs = other_core(whole)
     grads = unpack(ic.astype(jnp.int32)[None], whole, theirs)

time: 263 us -> 270 us (1.027)
  local copies, waits for them, and re-layouts: 22.9 us -> 27.7 us
    reduce_scatter x1, waiting for transfers between devices: 0.02 us -> 10.6 us  [body(): last = lax.psum_scatter(last, 'z', scatter_dimension=0).astype(WIDE)]
    all_to_all x8, waiting for transfers between devices: 75.9 us -> 71.2 us  [swap(): return lax.all_to_all(value, axis, 0, 0, tiled=True)]
    ppermute x2, starting transfers between devices: 14 us -> 11.1 us  [other_core(): return lax.ppermute(value, 'c', [(0, 1), (1, 0)])]
  transfers between devices with their start and end apart: 15 -> 16, of which waited for: 11 -> 10; matrix products, arithmetic and copies ran while one was open for 12% -> 14% of each run, Pallas kernels for 8% -> 8%
where the time goes in v2:
time: 270 us; the launch traced here: 268 us
  waiting for transfers between devices  87.3 us (32%)
  starting transfers between devices  45.1 us (17%)
  Pallas kernels  37.6 us (14%)
  blocking collectives  34.2 us (13%)
  local copies, waits for them, and re-layouts  27.7 us (10%)
  other arithmetic  19.3 us (7%)
  between operations  14.6 us (5%)
    all_to_all x8, waiting for transfers between devices, swap(): return lax.all_to_all(value, axis, 0, 0, tiled=True)  71.2 us
    all_to_all x2, blocking collectives, swap(): return lax.all_to_all(value, axis, 0, 0, tiled=True)  34.2 us
    all_to_all x8, starting transfers between devices, swap(): return lax.all_to_all(value, axis, 0, 0, tiled=True)  33.6 us
    ppermute x2, starting transfers between devices, other_core(): return lax.ppermute(value, 'c', [(0, 1), (1, 0)])  11.1 us
    reduce_scatter x1, waiting for transfers between devices, body(): last = lax.psum_scatter(last, 'z', scatter_dimension=0).astype(WIDE)  10.6 us
    pallas_call x1, Pallas kernels, attend_backward(): pl.pallas_call(backward_kernel, out_shape=(jax.ShapeDtypeStruct((4 * TOK,...  9.97 us
    pallas_call x1, Pallas kernels, feed_forward(): pl.pallas_call(ffn_kernel, out_shape=(jax.ShapeDtypeStruct((TOK, D), WIDE...  9.06 us
    pallas_call x1, Pallas kernels, attend_forward(): pl.pallas_call(forward_kernel, out_shape=(jax.ShapeDtypeStruct((4, 4 * TO...  6.47 us
  transfers between devices with their start and end apart: 16, of which 10 were waited for; matrix products, arithmetic and copies ran while one was open for 14% of the time, Pallas kernels for 8%

profile of v2, /device:TPU:1, one launch (start us, length us, event | category | flops | bytes accessed | tf_op | source)
XLA Modules:
  0.0 268.0 jit_solution(17068453708149053278)
XLA Ops:
  14.4 23.3 %all_to_all.50.early_ref = bf16[4,224,768]{2,1,0:T(8,128)(2,1)S(1)} all-to-all(bf16[4,224,768]{2,1,0:T(8,128)(2,1)} %get-tuple-element.48), channel_id=1, replica_groups=mesh['x'=4,'c'=2,'z'=4,'y'=4] {'z'}, dimensions={0} | all-to-all | bytes 2752512 | tf_op jit(solution)/shard_map/all_to_all | solution.py:537
  39.5 3.9 %all-gather.8.cloned.1.call-done = bf16[960,768]{1,0:T(8,128)(2,1)} async-done(((bf16[240,768]{1,0:T(8,128)(2,1)}), bf16[960,768]{1,0:T(8,128)(2,1)}) %all-gather.8.cloned.1.call-update) | async-done | bytes 1474576 | tf_op jit(solution)/shard_map/all_gather | solution.py:611
  46.3 4.2 %all-to-all-start.1 = ((bf16[4,4,48,640]{3,2,1,0:T(8,128)(2,1)}), bf16[4,4,48,640]{3,2,1,0:T(8,128)(2,1)}, u32[]{:S(2)}, u32[]{:S(2)}) async-start(bf16[4,4,48,640]{3,2,1,0:T(8,128)(2,1)} %broadcast_in_dim.50), calls=%async_computation.1 | async-start | bytes 1966080 | tf_op jit(solution)/shard_map/all_to_all | solution.py:537
  50.5 13.8 %all-to-all-done.1 = bf16[4,4,48,640]{3,2,1,0:T(8,128)(2,1)} async-done(((bf16[4,4,48,640]{3,2,1,0:T(8,128)(2,1)}), bf16[4,4,48,640]{3,2,1,0:T(8,128)(2,1)}, u32[]{:S(2)}, u32[]{:S(2)}) %all-to-all-start.1) | async-done | bytes 983072 | tf_op jit(solution)/shard_map/all_to_all | solution.py:537
  73.0 4.5 %all-to-all-start.2 = ((bf16[4,512,384]{2,1,0:T(8,128)(2,1)}), bf16[4,512,384]{2,1,0:T(8,128)(2,1)}, u32[]{:S(2)}, u32[]{:S(2)}) async-start(bf16[4,512,384]{2,1,0:T(8,128)(2,1)} %broadcast_in_dim.51), calls=%async_computation.2 | async-start | bytes 3145728 | tf_op jit(solution)/shard_map/all_to_all | solution.py:537
  82.7 14.0 %all-to-all-done.2.kv_ref = bf16[4,512,384]{2,1,0:T(8,128)(2,1)} async-done(((bf16[4,512,384]{2,1,0:T(8,128)(2,1)}), bf16[4,512,384]{2,1,0:T(8,128)(2,1)}, u32[]{:S(2)}, u32[]{:S(2)}) %all-to-all-start.2) | async-done | bytes 1572896 | tf_op jit(solution)/shard_map/all_to_all | solution.py:537
  96.7 6.5 %shard_map.272 = (bf16[4,512,192]{2,1,0:T(8,128)(2,1)S(1)}, f32[8,512]{1,0:T(8,128)S(1)}) custom-call(bf16[512,192]{1,0:T(8,128)(2,1)S(1)} %fusion.6.q_ref, bf16[4,512,384]{2,1,0:T(8,128)(2,1)} %all-to-all-done.2.kv_ref, s32[8,512]{1,0:T(8,128)S(1)} %add_add_fusion.bound_ref), custom_call_target="tpu_custom_call" | custom-call | flops 1000000000 | bytes 4000000 | tf_op jit(solution)/shard_map/pallas_call | solution.py:382
  104.4 4.1 %all-to-all-start.3 = ((bf16[4,512,192]{1,2,0:T(8,128)(2,1)}), bf16[4,512,192]{1,2,0:T(8,128)(2,1)S(1)}, u32[]{:S(2)}, u32[]{:S(2)}) async-start(bf16[4,512,192]{1,2,0:T(8,128)(2,1)} %copy.62), calls=%async_computation.3 | async-start | bytes 1572864 | tf_op jit(solution)/shard_map/all_to_all | solution.py:537
  110.6 6.2 %all-to-all-done.3 = bf16[4,512,192]{1,2,0:T(8,128)(2,1)S(1)} async-done(((bf16[4,512,192]{1,2,0:T(8,128)(2,1)}), bf16[4,512,192]{1,2,0:T(8,128)(2,1)S(1)}, u32[]{:S(2)}, u32[]{:S(2)}) %all-to-all-start.3) | async-done | bytes 786464 | tf_op jit(solution)/shard_map/all_to_all | solution.py:537
  118.1 9.1 %shard_map.273 = (f32[128,768]{1,0:T(8,128)}, bf16[512,768]{1,0:T(8,128)(2,1)}, bf16[512,768]{1,0:T(8,128)(2,1)}, bf16[512,768]{1,0:T(8,128)(2,1)}, bf16[512,768...) custom-call(s32[1]{0:T(128)} %bitcast.own_ref, bf16[4,224,768]{2,1,0:T(8,128)(2,1)} %copy-done, ...), custom_call_target="tpu_custom_call" | custom-call | flops 4000000000 | bytes 12000000 | tf_op jit(solution)/shard_map/pallas_call | solution.py:418
  127.2 4.4 %all-to-all-start.4 = ((bf16[4,128,768]{2,1,0:T(8,128)(2,1)}), bf16[4,128,768]{2,1,0:T(8,128)(2,1)}, u32[]{:S(2)}, u32[]{:S(2)}) async-start(bf16[4,128,768]{2,1,0:T(8,128)(2,1)} %bitcast.93), calls=%async_computation.4 | async-start | bytes 1572864 | tf_op jit(solution)/shard_map/all_to_all | solution.py:537
  132.1 7.9 %all-to-all-done.4 = bf16[4,128,768]{2,1,0:T(8,128)(2,1)} async-done(((bf16[4,128,768]{2,1,0:T(8,128)(2,1)}), bf16[4,128,768]{2,1,0:T(8,128)(2,1)}, u32[]{:S(2)}, u32[]{:S(2)}) %all-to-all-start.4) | async-done | bytes 786464 | tf_op jit(solution)/shard_map/all_to_all | solution.py:537
  142.5 10.9 %all_to_all.51 = bf16[4,128,768]{2,1,0:T(8,128)(2,1)S(1)} all-to-all(bf16[4,128,768]{2,1,0:T(8,128)(2,1)S(1)} %broadcast_in_dim.87), channel_id=1, replica_groups=mesh['x'=4,'c'=2,'z'=4,'y'=4] {'z'}, dimensions={0} | all-to-all | bytes 1572864 | tf_op jit(solution)/shard_map/all_to_all | solution.py:537
  158.3 10.0 %shard_map.274 = (bf16[512,192]{1,0:T(8,128)(2,1)S(1)}, bf16[4,512,384]{2,1,0:T(8,128)(2,1)S(1)}) custom-call(bf16[512,192]{1,0:T(8,128)(2,1)S(1)} %fusion.6.q_ref, bf16[4,512,384]{2,1,0:T(8,128)(2,1)} %all-to-all-done.2.kv_ref, s32[8,512]{1,0:T(8,128)S(1)} %add_add_fusion.bound_ref, f32[8,512]{1,0:T(8,128)S(1)} %get-tuple-element.55.lse_ref, ...), custom_call_target="tpu_custom_call" | custom-call | flops 2500000000 | bytes 6000000 | tf_op jit(solution)/shard_map/pallas_call | solution.py:398
  170.1 4.5 %all-to-all-start.6 = ((bf16[4,512,384]{2,1,0:T(8,128)(2,1)}), bf16[4,512,384]{2,1,0:T(8,128)(2,1)}, u32[]{:S(2)}, u32[]{:S(2)}) async-start(bf16[4,512,384]{2,1,0:T(8,128)(2,1)} %copy-done.4), calls=%async_computation.6 | async-start | bytes 3145728 | tf_op jit(solution)/shard_map/all_to_all | solution.py:537
  177.2 10.1 %all-to-all-done.6.moved_ref = bf16[4,512,384]{2,1,0:T(8,128)(2,1)} async-done(((bf16[4,512,384]{2,1,0:T(8,128)(2,1)}), bf16[4,512,384]{2,1,0:T(8,128)(2,1)}, u32[]{:S(2)}, u32[]{:S(2)}) %all-to-all-start.6) | async-done | bytes 1572896 | tf_op jit(solution)/shard_map/all_to_all | solution.py:537
  188.9 4.3 %shard_map.275 = (bf16[512,768]{1,0:T(8,128)(2,1)S(1)}, bf16[2,4,192,384]{3,2,1,0:T(8,128)(2,1)}) custom-call(s32[1]{0:T(128)} %bitcast.own_ref, bf16[4,512,384]{2,1,0:T(8,128)(2,1)} %all-to-all-done.6.moved_ref, bf16[512,192]{1,0:T(8,128)(2,1)S(1)} %copy-done.11, bf16[768,576]{1,0:T(8,128)(2,1)S(1)} %bitcast.82, ...), custom_call_target="tpu_custom_call" | custom-call | flops 1000000000 | bytes 7000000 | tf_op jit(solution)/shard_map/pallas_call | solution.py:464
  195.3 10.3 %collective-permute-start = (bf16[4,192,384]{2,1,0:T(8,128)(2,1)S(1)}, bf16[4,192,384]{2,1,0:T(8,128)(2,1)S(1)}, u32[]{:S(2)}, u32[]{:S(2)}) collective-permute-start(bf16[4,192,384]{2,1,0:T(8,128)(2,1)S(1)} %dynamic-slice_bitcast_fusion), channel_id=1, source_target_pairs={{0,16},{16,0},{1,17},{17,1},{2,18},{18,2},{3,19},{19,3},{4,20},{20... | collective-permute-start | bytes 1769480 | tf_op jit(solution)/shard_map/ppermute | solution.py:549
  210.6 3.5 %all-to-all-start.7 = ((bf16[4,192,384]{2,1,0:T(8,128)(2,1)}), bf16[4,192,384]{2,1,0:T(8,128)(2,1)S(1)}, u32[]{:S(2)}, u32[]{:S(2)}) async-start(bf16[4,192,384]{2,1,0:T(8,128)(2,1)} %fusion.1), calls=%async_computation.10 | async-start | bytes 1179648 | tf_op jit(solution)/shard_map/all_to_all | solution.py:537
  214.1 12.0 %all-to-all-done.7 = bf16[4,192,384]{2,1,0:T(8,128)(2,1)S(1)} async-done(((bf16[4,192,384]{2,1,0:T(8,128)(2,1)}), bf16[4,192,384]{2,1,0:T(8,128)(2,1)S(1)}, u32[]{:S(2)}, u32[]{:S(2)}) %all-to-all-start.7) | async-done | bytes 589856 | tf_op jit(solution)/shard_map/all_to_all | solution.py:537
  228.0 4.7 %all-to-all-start.8 = ((bf16[16,32,384]{2,1,0:T(8,128)(2,1)}), bf16[16,32,384]{2,1,0:T(8,128)(2,1)S(1)}, u32[]{:S(2)}, u32[]{:S(2)}) async-start(bf16[16,32,384]{2,1,0:T(8,128)(2,1)} %bitcast.43), calls=%async_computation.11 | async-start | bytes 786432 | tf_op jit(solution)/shard_map/all_to_all | solution.py:537
  233.5 7.2 %all-to-all-done.8 = bf16[16,32,384]{2,1,0:T(8,128)(2,1)S(1)} async-done(((bf16[16,32,384]{2,1,0:T(8,128)(2,1)}), bf16[16,32,384]{2,1,0:T(8,128)(2,1)S(1)}, u32[]{:S(2)}, u32[]{:S(2)}) %all-to-all-start.8) | async-done | bytes 393248 | tf_op jit(solution)/shard_map/all_to_all | solution.py:537
  241.7 3.6 %all-to-all-start.9 = ((bf16[4,192,384]{2,1,0:T(8,128)(2,1)}), bf16[4,192,384]{2,1,0:T(8,128)(2,1)S(1)}, u32[]{:S(2)}, u32[]{:S(2)}) async-start(bf16[4,192,384]{2,1,0:T(8,128)(2,1)} %broadcast_in_dim.93), calls=%async_computation.12 | async-start | bytes 1179648 | tf_op jit(solution)/shard_map/all_to_all | solution.py:537
  245.4 10.6 %reduce-scatter.4.cloned.1.call-done = bf16[1,128,1536]{2,1,0:T(8,128)(2,1)} async-done(((bf16[4,128,1536]{2,1,0:T(8,128)(2,1)}), bf16[1,128,1536]{2,1,0:T(8,128)(2,1)}) %reduce-scatter.4.cloned.1.call-update) | async-done | bytes 393232 | tf_op jit(solution)/shard_map/reduce_scatter | solution.py:682
  (146 shorter events, 59.9 us)
Async XLA Ops:
  7.2 36.2 %all-gather.8.cloned.1.call-start = ((), (), s32[]{:S(2)}) async-start(), calls=%async_computation.17 | async-start | bytes 1843200 | tf_op jit(solution)/shard_map/all_gather | solution.py:611
  14.3 64.0 %all-gather.10.cloned.1.call-start = ((), (), s32[]{:S(2)}) async-start(), calls=%async_computation.18 | async-start | bytes 2457600 | tf_op jit(solution)/shard_map/all_gather | solution.py:613
  37.7 42.5 %copy-start = (bf16[4,224,768]{2,1,0:T(8,128)(2,1)}, bf16[4,224,768]{2,1,0:T(8,128)(2,1)S(1)}, u32[]{:S(2)}) copy-start(bf16[4,224,768]{2,1,0:T(8,128)(2,1)S(1)} %all_to_all.50.early_ref) | copy-start | bytes 4128772
  46.3 18.0 %all-to-all-start.1 = ((bf16[4,4,48,640]{3,2,1,0:T(8,128)(2,1)}), bf16[4,4,48,640]{3,2,1,0:T(8,128)(2,1)}, u32[]{:S(2)}, u32[]{:S(2)}) async-start(bf16[4,4,48,640]{3,2,1,0:T(8,128)(2,1)} %broadcast_in_dim.50), calls=%async_computation.1 | async-start | bytes 1966080 | tf_op jit(solution)/shard_map/all_to_all | solution.py:537
  73.0 23.7 %all-to-all-start.2 = ((bf16[4,512,384]{2,1,0:T(8,128)(2,1)}), bf16[4,512,384]{2,1,0:T(8,128)(2,1)}, u32[]{:S(2)}, u32[]{:S(2)}) async-start(bf16[4,512,384]{2,1,0:T(8,128)(2,1)} %broadcast_in_dim.51), calls=%async_computation.2 | async-start | bytes 3145728 | tf_op jit(solution)/shard_map/all_to_all | solution.py:537
  77.5 40.7 %all-gather.6.cloned.1.call-start = ((), (), s32[]{:S(2)}) async-start(), calls=%async_computation.13 | async-start | bytes 1474560 | tf_op jit(solution)/shard_map/all_gather | solution.py:617
  104.4 12.5 %all-to-all-start.3 = ((bf16[4,512,192]{1,2,0:T(8,128)(2,1)}), bf16[4,512,192]{1,2,0:T(8,128)(2,1)S(1)}, u32[]{:S(2)}, u32[]{:S(2)}) async-start(bf16[4,512,192]{1,2,0:T(8,128)(2,1)} %copy.62), calls=%async_computation.3 | async-start | bytes 1572864 | tf_op jit(solution)/shard_map/all_to_all | solution.py:537
  127.2 12.8 %all-to-all-start.4 = ((bf16[4,128,768]{2,1,0:T(8,128)(2,1)}), bf16[4,128,768]{2,1,0:T(8,128)(2,1)}, u32[]{:S(2)}, u32[]{:S(2)}) async-start(bf16[4,128,768]{2,1,0:T(8,128)(2,1)} %bitcast.93), calls=%async_computation.4 | async-start | bytes 1572864 | tf_op jit(solution)/shard_map/all_to_all | solution.py:537
  131.6 74.0 %reduce-scatter.6.cloned.1.call-start = ((), (), s32[]{:S(2)}) async-start(), calls=%async_computation.15 | async-start | bytes 3538944 | tf_op jit(solution)/shard_map/reduce_scatter | solution.py:661
  141.3 12.1 %copy-start.7 = (bf16[512,768]{1,0:T(8,128)(2,1)S(1)}, bf16[512,768]{1,0:T(8,128)(2,1)}, u32[]{:S(2)}) copy-start(bf16[512,768]{1,0:T(8,128)(2,1)} %get-tuple-element.65.d_up_ref) | copy-start | bytes 2359300
  141.5 11.9 %copy-start.5 = (bf16[512,768]{1,0:T(8,128)(2,1)S(1)}, bf16[512,768]{1,0:T(8,128)(2,1)}, u32[]{:S(2)}) copy-start(bf16[512,768]{1,0:T(8,128)(2,1)} %get-tuple-element.64.normed_ref) | copy-start | bytes 2359300
  141.5 11.9 %copy-start.6 = (bf16[512,768]{1,0:T(8,128)(2,1)S(1)}, bf16[512,768]{1,0:T(8,128)(2,1)}, u32[]{:S(2)}) copy-start(bf16[512,768]{1,0:T(8,128)(2,1)} %get-tuple-element.66.act_ref) | copy-start | bytes 2359300
  170.1 17.1 %all-to-all-start.6 = ((bf16[4,512,384]{2,1,0:T(8,128)(2,1)}), bf16[4,512,384]{2,1,0:T(8,128)(2,1)}, u32[]{:S(2)}, u32[]{:S(2)}) async-start(bf16[4,512,384]{2,1,0:T(8,128)(2,1)} %copy-done.4), calls=%async_computation.6 | async-start | bytes 3145728 | tf_op jit(solution)/shard_map/all_to_all | solution.py:537
  174.6 51.6 %reduce-scatter.8.cloned.1.call-start = ((), (), s32[]{:S(2)}) async-start(), calls=%async_computation.16 | async-start | bytes 491520 | tf_op jit(solution)/shard_map/reduce_scatter | solution.py:663
  194.1 15.2 %copy-start.9 = (bf16[512,768]{1,0:T(8,128)(2,1)S(1)}, bf16[512,768]{1,0:T(8,128)(2,1)}, u32[]{:S(2)}) copy-start(bf16[512,768]{1,0:T(8,128)(2,1)} %copy-done.8) | copy-start | bytes 2359300
  194.1 15.2 %copy-start.16 = (bf16[512,768]{1,0:T(8,128)(2,1)S(1)}, bf16[512,768]{1,0:T(8,128)(2,1)}, u32[]{:S(2)}) copy-start(bf16[512,768]{1,0:T(8,128)(2,1)} %get-tuple-element.63) | copy-start | bytes 2359300
  195.3 11.9 %collective-permute-start = (bf16[4,192,384]{2,1,0:T(8,128)(2,1)S(1)}, bf16[4,192,384]{2,1,0:T(8,128)(2,1)S(1)}, u32[]{:S(2)}, u32[]{:S(2)}) collective-permute-start(bf16[4,192,384]{2,1,0:T(8,128)(2,1)S(1)} %dynamic-slice_bitcast_fusion), channel_id=1, source_target_pairs={{0,16},{16,0},{1,17},{17,1},{2,18},{18,2},{3,19},{19,3},{4,20},{20... | collective-permute-start | bytes 1769480 | tf_op jit(solution)/shard_map/ppermute | solution.py:549
  205.7 50.3 %reduce-scatter.4.cloned.1.call-start = ((), (), s32[]{:S(2)}) async-start(), calls=%async_computation.14 | async-start | bytes 1966080 | tf_op jit(solution)/shard_map/reduce_scatter | solution.py:682
  210.6 15.5 %all-to-all-start.7 = ((bf16[4,192,384]{2,1,0:T(8,128)(2,1)}), bf16[4,192,384]{2,1,0:T(8,128)(2,1)S(1)}, u32[]{:S(2)}, u32[]{:S(2)}) async-start(bf16[4,192,384]{2,1,0:T(8,128)(2,1)} %fusion.1), calls=%async_computation.10 | async-start | bytes 1179648 | tf_op jit(solution)/shard_map/all_to_all | solution.py:537
  228.0 12.7 %all-to-all-start.8 = ((bf16[16,32,384]{2,1,0:T(8,128)(2,1)}), bf16[16,32,384]{2,1,0:T(8,128)(2,1)S(1)}, u32[]{:S(2)}, u32[]{:S(2)}) async-start(bf16[16,32,384]{2,1,0:T(8,128)(2,1)} %bitcast.43), calls=%async_computation.11 | async-start | bytes 786432 | tf_op jit(solution)/shard_map/all_to_all | solution.py:537
  240.9 16.1 %copy-start.15 = (f32[512,768]{1,0:T(8,128)S(1)}, f32[512,768]{1,0:T(8,128)}, u32[]{:S(2)}) copy-start(f32[512,768]{1,0:T(8,128)} %get-tuple-element.93) | copy-start | bytes 4718596
  241.7 16.2 %copy-start.14 = (f32[128,768]{1,0:T(8,128)S(1)}, f32[128,768]{1,0:T(8,128)}, u32[]{:S(2)}) copy-start(f32[128,768]{1,0:T(8,128)} %get-tuple-element.54) | copy-start | bytes 1179652
  241.7 15.4 %all-to-all-start.9 = ((bf16[4,192,384]{2,1,0:T(8,128)(2,1)}), bf16[4,192,384]{2,1,0:T(8,128)(2,1)S(1)}, u32[]{:S(2)}, u32[]{:S(2)}) async-start(bf16[4,192,384]{2,1,0:T(8,128)(2,1)} %broadcast_in_dim.93), calls=%async_computation.12 | async-start | bytes 1179648 | tf_op jit(solution)/shard_map/all_to_all | solution.py:537
  257.1 2.7 collective-permute-start.1
  (14 other events, 49.0 us)
Sparse Core Ops, SparseCore 0:
  14.5 28.8 all-gather.7
  45.6 30.4 all-gather.9
  80.5 27.4 all-gather.5
  156.9 38.5 reduce-scatter.5
  205.8 16.7 reduce-scatter.7
  225.0 30.8 reduce-scatter.3

commit v3 on v1

--- a/solution.py
+++ b/solution.py
@@ -405,7 +405,7 @@
             pltpu.VMEM((4 * CHUNK, 4 * TOK), LOW),
             pltpu.VMEM((4 * CHUNK, 4 * TOK), LOW),
         ],
-        compiler_params=PARAMS,
+        compiler_params=WHOLE,
         cost_estimate=pl.CostEstimate(
             flops=2_500_000_000, bytes_accessed=6_000_000, transcendentals=2_000_000
         ),
@@ -451,7 +451,7 @@
         in_specs=[VMEM] * 6,
         out_specs=VMEM,
         scratch_shapes=[pltpu.VMEM((4 * TOK, D), LOW)],
-        compiler_params=PARAMS,
+        compiler_params=WHOLE,
         cost_estimate=pl.CostEstimate(
             flops=1_400_000_000, bytes_accessed=9_000_000, transcendentals=0
         ),
@@ -468,7 +468,7 @@
         in_specs=[pl.BlockSpec(memory_space=pltpu.SMEM)] + [VMEM] * 8,
         out_specs=(VMEM, VMEM),
         scratch_shapes=[pltpu.VMEM((4 * TOK, D), WIDE)],
-        compiler_params=PARAMS,
+        compiler_params=WHOLE,
         cost_estimate=pl.CostEstimate(
             flops=1_000_000_000, bytes_accessed=7_000_000, transcendentals=0
         ),

time: 263 us -> 263 us (level)
  Pallas kernels: 36.5 us -> 41.1 us
  waiting for transfers between devices: 85.5 us -> 81.8 us
  starting transfers between devices: 46.4 us -> 43.4 us
    all_to_all x8, waiting for transfers between devices: 75.9 us -> 71.4 us  [swap(): return lax.all_to_all(value, axis, 0, 0, tiled=True)]
    unnamed x45 -> x49, local copies, waits for them, and re-layouts: 6.22 us -> 4.15 us
  transfers between devices with their start and end apart: 15 -> 15, of which waited for: 11 -> 11; matrix products, arithmetic and copies ran while one was open for 12% -> 14% of each run, Pallas kernels for 8% -> 8%
where the time goes in v3:
time: 263 us; the launch traced here: 262 us
  waiting for transfers between devices  81.8 us (31%)
  starting transfers between devices  43.4 us (17%)
  Pallas kernels  41.1 us (16%)
  blocking collectives  34.8 us (13%)
  local copies, waits for them, and re-layouts  24.5 us (9%)
  other arithmetic  19.8 us (8%)
  between operations  14.4 us (5%)
    all_to_all x8, waiting for transfers between devices, swap(): return lax.all_to_all(value, axis, 0, 0, tiled=True)  71.4 us
    all_to_all x2, blocking collectives, swap(): return lax.all_to_all(value, axis, 0, 0, tiled=True)  34.8 us
    all_to_all x8, starting transfers between devices, swap(): return lax.all_to_all(value, axis, 0, 0, tiled=True)  30.2 us
    ppermute x2, starting transfers between devices, other_core(): return lax.ppermute(value, 'c', [(0, 1), (1, 0)])  12.7 us
    pallas_call x1, Pallas kernels, attend_backward(): pl.pallas_call(backward_kernel, out_shape=(jax.ShapeDtypeStruct((4 * TOK,...  11.3 us
    pallas_call x1, Pallas kernels, feed_forward(): pl.pallas_call(ffn_kernel, out_shape=(jax.ShapeDtypeStruct((TOK, D), WIDE...  9.05 us
    pallas_call x1, Pallas kernels, weight_grads(): pl.pallas_call(grad_kernel, out_shape=jax.ShapeDtypeStruct((8, 4 * TOK, D...  5.77 us
    all_gather x1, waiting for transfers between devices, body(): plain = lax.all_gather(plain, 'y')  5.63 us
  transfers between devices with their start and end apart: 15, of which 11 were waited for; matrix products, arithmetic and copies ran while one was open for 14% of the time, Pallas kernels for 8%

profile of v3, /device:TPU:1, one launch (start us, length us, event | category | flops | bytes accessed | tf_op | source)
XLA Modules:
  0.0 261.6 jit_solution(1981185021940529647)
XLA Ops:
  14.4 23.3 %all_to_all.50.early_ref = bf16[4,224,768]{2,1,0:T(8,128)(2,1)S(1)} all-to-all(bf16[4,224,768]{2,1,0:T(8,128)(2,1)} %get-tuple-element.48), channel_id=1, replica_groups=mesh['x'=4,'c'=2,'z'=4,'y'=4] {'z'}, dimensions={0} | all-to-all | bytes 2752512 | tf_op jit(solution)/shard_map/all_to_all | solution.py:535
  37.7 5.6 %all-gather.8.cloned.1.call-done = bf16[960,768]{1,0:T(8,128)(2,1)} async-done(((bf16[240,768]{1,0:T(8,128)(2,1)}), bf16[960,768]{1,0:T(8,128)(2,1)}) %all-gather.8.cloned.1.call-update) | async-done | bytes 1474576 | tf_op jit(solution)/shard_map/all_gather | solution.py:606
  46.2 3.5 %all-to-all-start.1 = ((bf16[4,4,48,640]{3,2,1,0:T(8,128)(2,1)}), bf16[4,4,48,640]{3,2,1,0:T(8,128)(2,1)S(1)}, u32[]{:S(2)}, u32[]{:S(2)}) async-start(bf16[4,4,48,640]{3,2,1,0:T(8,128)(2,1)} %broadcast_in_dim.52), calls=%async_computation.1 | async-start | bytes 1966080 | tf_op jit(solution)/shard_map/all_to_all | solution.py:535
  51.5 11.9 %all-to-all-done.1 = bf16[4,4,48,640]{3,2,1,0:T(8,128)(2,1)S(1)} async-done(((bf16[4,4,48,640]{3,2,1,0:T(8,128)(2,1)}), bf16[4,4,48,640]{3,2,1,0:T(8,128)(2,1)S(1)}, u32[]{:S(2)}, u32[]{:S(2)}) %all-to-all-start.1) | async-done | bytes 983072 | tf_op jit(solution)/shard_map/all_to_all | solution.py:535
  68.8 3.6 %all-to-all-start.2 = ((bf16[4,512,384]{2,1,0:T(8,128)(2,1)}), bf16[4,512,384]{2,1,0:T(8,128)(2,1)S(1)}, u32[]{:S(2)}, u32[]{:S(2)}) async-start(bf16[4,512,384]{2,1,0:T(8,128)(2,1)} %broadcast_in_dim.53), calls=%async_computation.2 | async-start | bytes 3145728 | tf_op jit(solution)/shard_map/all_to_all | solution.py:535
  84.4 7.2 %all-to-all-done.2.kv_ref = bf16[4,512,384]{2,1,0:T(8,128)(2,1)S(1)} async-done(((bf16[4,512,384]{2,1,0:T(8,128)(2,1)}), bf16[4,512,384]{2,1,0:T(8,128)(2,1)S(1)}, u32[]{:S(2)}, u32[]{:S(2)}) %all-to-all-start.2) | async-done | bytes 1572896 | tf_op jit(solution)/shard_map/all_to_all | solution.py:535
  91.5 5.0 %shard_map.272 = (bf16[512,192]{1,0:T(8,128)(2,1)S(1)}, f32[8,512]{1,0:T(8,128)S(1)}) custom-call(bf16[512,192]{1,0:T(8,128)(2,1)S(1)} %fusion.6.q_ref, bf16[4,512,384]{2,1,0:T(8,128)(2,1)S(1)} %all-to-all-done.2.kv_ref, s32[8,512]{1,0:T(8,128)S(1)} %add_add_fusion.bound_ref), custom_call_target="tpu_custom_call" | custom-call | flops 1000000000 | bytes 4000000 | tf_op jit(solution)/shard_map/pallas_call | solution.py:380
  98.2 4.1 %all-to-all-start.3 = ((bf16[4,512,192]{1,2,0:T(8,128)(2,1)}), bf16[4,512,192]{1,2,0:T(8,128)(2,1)S(1)}, u32[]{:S(2)}, u32[]{:S(2)}) async-start(bf16[4,512,192]{1,2,0:T(8,128)(2,1)} %broadcast_in_dim.93), calls=%async_computation.3 | async-start | bytes 1572864 | tf_op jit(solution)/shard_map/all_to_all | solution.py:535
  104.5 6.2 %all-to-all-done.3 = bf16[4,512,192]{1,2,0:T(8,128)(2,1)S(1)} async-done(((bf16[4,512,192]{1,2,0:T(8,128)(2,1)}), bf16[4,512,192]{1,2,0:T(8,128)(2,1)S(1)}, u32[]{:S(2)}, u32[]{:S(2)}) %all-to-all-start.3) | async-done | bytes 786464 | tf_op jit(solution)/shard_map/all_to_all | solution.py:535
  112.0 9.0 %shard_map.273 = (f32[128,768]{1,0:T(8,128)}, bf16[512,768]{1,0:T(8,128)(2,1)}, bf16[512,768]{1,0:T(8,128)(2,1)}, bf16[512,768]{1,0:T(8,128)(2,1)}, bf16[512,768...) custom-call(s32[1]{0:T(128)} %bitcast.own_ref, bf16[4,224,768]{2,1,0:T(8,128)(2,1)} %copy-done.5, ...), custom_call_target="tpu_custom_call" | custom-call | flops 4000000000 | bytes 12000000 | tf_op jit(solution)/shard_map/pallas_call | solution.py:416
  121.0 3.6 %all-to-all-start.4 = ((bf16[4,128,768]{2,1,0:T(8,128)(2,1)}), bf16[4,128,768]{2,1,0:T(8,128)(2,1)S(1)}, u32[]{:S(2)}, u32[]{:S(2)}) async-start(bf16[4,128,768]{2,1,0:T(8,128)(2,1)} %bitcast.93), calls=%async_computation.4 | async-start | bytes 1572864 | tf_op jit(solution)/shard_map/all_to_all | solution.py:535
  125.2 7.8 %all-to-all-done.4 = bf16[4,128,768]{2,1,0:T(8,128)(2,1)S(1)} async-done(((bf16[4,128,768]{2,1,0:T(8,128)(2,1)}), bf16[4,128,768]{2,1,0:T(8,128)(2,1)S(1)}, u32[]{:S(2)}, u32[]{:S(2)}) %all-to-all-start.4) | async-done | bytes 786464 | tf_op jit(solution)/shard_map/all_to_all | solution.py:535
  134.3 11.5 %all_to_all.51 = bf16[4,128,768]{2,1,0:T(8,128)(2,1)} all-to-all(bf16[4,128,768]{2,1,0:T(8,128)(2,1)S(1)} %broadcast_in_dim.94), channel_id=1, replica_groups=mesh['x'=4,'c'=2,'z'=4,'y'=4] {'z'}, dimensions={0} | all-to-all | bytes 1572864 | tf_op jit(solution)/shard_map/all_to_all | solution.py:535
  145.8 5.8 %shard_map.276 = bf16[8,512,384]{2,1,0:T(8,128)(2,1)} custom-call(bf16[512,768]{1,0:T(8,128)(2,1)} %get-tuple-element.64.normed_ref, bf16[512,768]{1,0:T(8,128)(2,1)} %get-tuple-element.65.d_up_ref, bf16[512,768]{1,0:T(8,128)(2,1)} %get-tuple-element.66.act_ref, bf16[4,320,768]{2,1,0:T(8,128)(2,1)} %bitcast.88, bf16[512,192]{1,0:T(8,128)(2,1)} %copy-done.1, ...), custom_call_target="tpu_custom_call" | custom-call | flops 1400000000 | bytes 9000000 | tf_op jit(solution)/shard_map/pallas_call | solution.py:448
  154.9 11.3 %shard_map.274 = (bf16[512,192]{1,0:T(8,128)(2,1)}, bf16[4,512,384]{2,1,0:T(8,128)(2,1)}) custom-call(bf16[512,192]{1,0:T(8,128)(2,1)} %copy-done.2, bf16[4,512,384]{2,1,0:T(8,128)(2,1)} %copy-done, s32[8,512]{1,0:T(8,128)} %copy-done.3, f32[8,512]{1,0:T(8,128)} %copy-done.4, bf16[512,192]{1,0:T(8,128)(2,1)} %copy.65.do_ref), custom_call_target="tpu_custom_call" | custom-call | flops 2500000000 | bytes 6000000 | tf_op jit(solution)/shard_map/pallas_call | solution.py:396
  166.2 3.7 %all-to-all-start.6 = ((bf16[4,512,384]{2,1,0:T(8,128)(2,1)}), bf16[4,512,384]{2,1,0:T(8,128)(2,1)S(1)}, u32[]{:S(2)}, u32[]{:S(2)}) async-start(bf16[4,512,384]{2,1,0:T(8,128)(2,1)} %get-tuple-element.57), calls=%async_computation.6 | async-start | bytes 3145728 | tf_op jit(solution)/shard_map/all_to_all | solution.py:535
  172.0 10.6 %all-to-all-done.6.moved_ref = bf16[4,512,384]{2,1,0:T(8,128)(2,1)S(1)} async-done(((bf16[4,512,384]{2,1,0:T(8,128)(2,1)}), bf16[4,512,384]{2,1,0:T(8,128)(2,1)S(1)}, u32[]{:S(2)}, u32[]{:S(2)}) %all-to-all-start.6) | async-done | bytes 1572896 | tf_op jit(solution)/shard_map/all_to_all | solution.py:535
  183.8 5.5 %shard_map.275 = (bf16[512,768]{1,0:T(8,128)(2,1)}, bf16[2,4,192,384]{3,2,1,0:T(8,128)(2,1)}) custom-call(s32[1]{0:T(128)} %bitcast.own_ref, bf16[4,512,384]{2,1,0:T(8,128)(2,1)} %copy-done.10, bf16[512,192]{1,0:T(8,128)(2,1)} %get-tuple-element.58.query_ref, bf16[768,576]{1,0:T(8,128)(2,1)} %bitcast.82, bf16[512,768]{1,0:T(8,128)(2,1)} %get-tuple-element.94.normed_ref, ...), custom_call_target="tpu_custom_call" | custom-call | flops 1000000000 | bytes 7000000 | tf_op jit(solution)/shard_map/pallas_call | solution.py:462
  190.6 8.8 %collective-permute-start = (bf16[4,192,384]{2,1,0:T(8,128)(2,1)S(1)}, bf16[4,192,384]{2,1,0:T(8,128)(2,1)S(1)}, u32[]{:S(2)}, u32[]{:S(2)}) collective-permute-start(bf16[4,192,384]{2,1,0:T(8,128)(2,1)S(1)} %dynamic-slice_bitcast_fusion), channel_id=1, source_target_pairs={{0,16},{16,0},{1,17},{17,1},{2,18},{18,2},{3,19},{19,3},{4,20},{20... | collective-permute-start | bytes 1769480 | tf_op jit(solution)/shard_map/ppermute | solution.py:547
  208.2 14.1 %all-to-all-done.7 = bf16[4,320,384]{2,1,0:T(8,128)(2,1)S(1)} async-done(((bf16[4,320,384]{2,1,0:T(8,128)(2,1)}), bf16[4,320,384]{2,1,0:T(8,128)(2,1)S(1)}, u32[]{:S(2)}, u32[]{:S(2)}) %all-to-all-start.7) | async-done | bytes 983072 | tf_op jit(solution)/shard_map/all_to_all | solution.py:535
  223.5 4.7 %all-to-all-start.8 = ((bf16[16,32,384]{2,1,0:T(8,128)(2,1)}), bf16[16,32,384]{2,1,0:T(8,128)(2,1)S(1)}, u32[]{:S(2)}, u32[]{:S(2)}) async-start(bf16[16,32,384]{2,1,0:T(8,128)(2,1)} %bitcast.43), calls=%async_computation.10 | async-start | bytes 786432 | tf_op jit(solution)/shard_map/all_to_all | solution.py:535
  228.9 7.5 %all-to-all-done.8 = bf16[16,32,384]{2,1,0:T(8,128)(2,1)S(1)} async-done(((bf16[16,32,384]{2,1,0:T(8,128)(2,1)}), bf16[16,32,384]{2,1,0:T(8,128)(2,1)S(1)}, u32[]{:S(2)}, u32[]{:S(2)}) %all-to-all-start.8) | async-done | bytes 393248 | tf_op jit(solution)/shard_map/all_to_all | solution.py:535
  242.0 6.0 %all-to-all-done.9.mine_ref = bf16[4,192,384]{2,1,0:T(8,128)(2,1)S(1)} async-done(((bf16[4,192,384]{2,1,0:T(8,128)(2,1)}), bf16[4,192,384]{2,1,0:T(8,128)(2,1)S(1)}, u32[]{:S(2)}, u32[]{:S(2)}) %all-to-all-start.9) | async-done | bytes 589856 | tf_op jit(solution)/shard_map/all_to_all | solution.py:535
  248.1 3.8 %collective-permute-start.1 = (bf16[4,192,384]{2,1,0:T(8,128)(2,1)S(1)}, bf16[4,192,384]{2,1,0:T(8,128)(2,1)S(1)}, u32[]{:S(2)}, u32[]{:S(2)}) collective-permute-start(bf16[4,192,384]{2,1,0:T(8,128)(2,1)S(1)} %all-to-all-done.9.mine_ref), channel_id=1, source_target_pairs={{0,16},{16,0},{1,17},{17,1},{2,18},{18,2},{3,19},{19,3},{4,20},{20... | collective-permute-start | bytes 1769480 | tf_op jit(solution)/shard_map/ppermute | solution.py:547
  (150 shorter events, 63.0 us)
Async XLA Ops:
  7.2 36.2 %all-gather.8.cloned.1.call-start = ((), (), s32[]{:S(2)}) async-start(), calls=%async_computation.15 | async-start | bytes 1843200 | tf_op jit(solution)/shard_map/all_gather | solution.py:606
  14.3 62.5 %all-gather.10.cloned.1.call-start = ((), (), s32[]{:S(2)}) async-start(), calls=%async_computation.16 | async-start | bytes 2457600 | tf_op jit(solution)/shard_map/all_gather | solution.py:608
  37.7 43.8 %copy-start.5 = (bf16[4,224,768]{2,1,0:T(8,128)(2,1)}, bf16[4,224,768]{2,1,0:T(8,128)(2,1)S(1)}, u32[]{:S(2)}) copy-start(bf16[4,224,768]{2,1,0:T(8,128)(2,1)S(1)} %all_to_all.50.early_ref) | copy-start | bytes 4128772
  37.7 7.7 %copy-start.12 = (bf16[128,768]{1,0:T(8,128)(2,1)S(1)}, bf16[128,768]{1,0:T(8,128)(2,1)}, u32[]{:S(2)}) copy-start(bf16[128,768]{1,0:T(8,128)(2,1)} %cot_ref.1) | copy-start | bytes 589828
  46.2 17.2 %all-to-all-start.1 = ((bf16[4,4,48,640]{3,2,1,0:T(8,128)(2,1)}), bf16[4,4,48,640]{3,2,1,0:T(8,128)(2,1)S(1)}, u32[]{:S(2)}, u32[]{:S(2)}) async-start(bf16[4,4,48,640]{3,2,1,0:T(8,128)(2,1)} %broadcast_in_dim.52), calls=%async_computation.1 | async-start | bytes 1966080 | tf_op jit(solution)/shard_map/all_to_all | solution.py:535
  51.5 14.3 %copy-start.21 = (f32[4,128]{1,0:T(4,128)}, f32[4,128]{1,0:T(4,128)S(1)}, u32[]{:S(2)}) copy-start(f32[4,128]{1,0:T(4,128)S(1)} %get-tuple-element.104) | copy-start | bytes 6148
  68.8 22.7 %all-to-all-start.2 = ((bf16[4,512,384]{2,1,0:T(8,128)(2,1)}), bf16[4,512,384]{2,1,0:T(8,128)(2,1)S(1)}, u32[]{:S(2)}, u32[]{:S(2)}) async-start(bf16[4,512,384]{2,1,0:T(8,128)(2,1)} %broadcast_in_dim.53), calls=%async_computation.2 | async-start | bytes 3145728 | tf_op jit(solution)/shard_map/all_to_all | solution.py:535
  72.4 39.5 %all-gather.6.cloned.1.call-start = ((), (), s32[]{:S(2)}) async-start(), calls=%async_computation.12 | async-start | bytes 1474560 | tf_op jit(solution)/shard_map/all_gather | solution.py:612
  83.6 12.9 %copy-start.3 = (s32[8,512]{1,0:T(8,128)}, s32[8,512]{1,0:T(8,128)S(1)}, u32[]{:S(2)}) copy-start(s32[8,512]{1,0:T(8,128)S(1)} %add_add_fusion.bound_ref) | copy-start | bytes 49156
  84.3 12.2 %copy-start.2 = (bf16[512,192]{1,0:T(8,128)(2,1)}, bf16[512,192]{1,0:T(8,128)(2,1)S(1)}, u32[]{:S(2)}) copy-start(bf16[512,192]{1,0:T(8,128)(2,1)S(1)} %fusion.6.q_ref) | copy-start | bytes 589828
  98.2 12.4 %all-to-all-start.3 = ((bf16[4,512,192]{1,2,0:T(8,128)(2,1)}), bf16[4,512,192]{1,2,0:T(8,128)(2,1)S(1)}, u32[]{:S(2)}, u32[]{:S(2)}) async-start(bf16[4,512,192]{1,2,0:T(8,128)(2,1)} %broadcast_in_dim.93), calls=%async_computation.3 | async-start | bytes 1572864 | tf_op jit(solution)/shard_map/all_to_all | solution.py:535
  121.0 11.9 %all-to-all-start.4 = ((bf16[4,128,768]{2,1,0:T(8,128)(2,1)}), bf16[4,128,768]{2,1,0:T(8,128)(2,1)S(1)}, u32[]{:S(2)}, u32[]{:S(2)}) async-start(bf16[4,128,768]{2,1,0:T(8,128)(2,1)} %bitcast.93), calls=%async_computation.4 | async-start | bytes 1572864 | tf_op jit(solution)/shard_map/all_to_all | solution.py:535
  124.7 8.6 %copy-start.13 = (bf16[128,768]{1,0:T(8,128)(2,1)S(1)}, bf16[128,768]{1,0:T(8,128)(2,1)}, u32[]{:S(2)}) copy-start(bf16[128,768]{1,0:T(8,128)(2,1)} %cot_ref.1) | copy-start | bytes 589828
  124.7 77.9 %reduce-scatter.5.cloned.1.call-start = ((), (), s32[]{:S(2)}) async-start(), calls=%async_computation.14 | async-start | bytes 3538944 | tf_op jit(solution)/shard_map/reduce_scatter | solution.py:658
  134.2 17.3 %copy-start.14 = (bf16[128,768]{1,0:T(8,128)(2,1)}, bf16[128,768]{1,0:T(8,128)(2,1)S(1)}, u32[]{:S(2)}) copy-start(bf16[128,768]{1,0:T(8,128)(2,1)S(1)} %get-tuple-element.91.branch_ref) | copy-start | bytes 589828
  166.2 16.5 %all-to-all-start.6 = ((bf16[4,512,384]{2,1,0:T(8,128)(2,1)}), bf16[4,512,384]{2,1,0:T(8,128)(2,1)S(1)}, u32[]{:S(2)}, u32[]{:S(2)}) async-start(bf16[4,512,384]{2,1,0:T(8,128)(2,1)} %get-tuple-element.57), calls=%async_computation.6 | async-start | bytes 3145728 | tf_op jit(solution)/shard_map/all_to_all | solution.py:535
  169.9 70.9 %reduce-scatter.3.cloned.1.call-start = ((), (), s32[]{:S(2)}) async-start(), calls=%async_computation.13 | async-start | bytes 1966080 | tf_op jit(solution)/shard_map/reduce_scatter | solution.py:678
  189.3 11.8 %copy-start.15 = (bf16[2,4,192,384]{3,2,1,0:T(8,128)(2,1)S(1)}, bf16[2,4,192,384]{3,2,1,0:T(8,128)(2,1)}, u32[]{:S(2)}) copy-start(bf16[2,4,192,384]{3,2,1,0:T(8,128)(2,1)} %get-tuple-element.60) | copy-start | bytes 3538948
  189.3 11.9 %copy-start.16 = (bf16[512,768]{1,0:T(8,128)(2,1)S(1)}, bf16[512,768]{1,0:T(8,128)(2,1)}, u32[]{:S(2)}) copy-start(bf16[512,768]{1,0:T(8,128)(2,1)} %get-tuple-element.63) | copy-start | bytes 2359300
  190.6 10.5 %collective-permute-start = (bf16[4,192,384]{2,1,0:T(8,128)(2,1)S(1)}, bf16[4,192,384]{2,1,0:T(8,128)(2,1)S(1)}, u32[]{:S(2)}, u32[]{:S(2)}) collective-permute-start(bf16[4,192,384]{2,1,0:T(8,128)(2,1)S(1)} %dynamic-slice_bitcast_fusion), channel_id=1, source_target_pairs={{0,16},{16,0},{1,17},{17,1},{2,18},{18,2},{3,19},{19,3},{4,20},{20... | collective-permute-start | bytes 1769480 | tf_op jit(solution)/shard_map/ppermute | solution.py:547
  204.6 17.6 %all-to-all-start.7 = ((bf16[4,320,384]{2,1,0:T(8,128)(2,1)}), bf16[4,320,384]{2,1,0:T(8,128)(2,1)S(1)}, u32[]{:S(2)}, u32[]{:S(2)}) async-start(bf16[4,320,384]{2,1,0:T(8,128)(2,1)} %pad_maximum_fusion.1), calls=%async_computation.9 | async-start | bytes 1966080 | tf_op jit(solution)/shard_map/all_to_all | solution.py:535
  223.5 12.8 %all-to-all-start.8 = ((bf16[16,32,384]{2,1,0:T(8,128)(2,1)}), bf16[16,32,384]{2,1,0:T(8,128)(2,1)S(1)}, u32[]{:S(2)}, u32[]{:S(2)}) async-start(bf16[16,32,384]{2,1,0:T(8,128)(2,1)} %bitcast.43), calls=%async_computation.10 | async-start | bytes 786432 | tf_op jit(solution)/shard_map/all_to_all | solution.py:535
  237.3 10.8 %all-to-all-start.9 = ((bf16[4,192,384]{2,1,0:T(8,128)(2,1)}), bf16[4,192,384]{2,1,0:T(8,128)(2,1)S(1)}, u32[]{:S(2)}, u32[]{:S(2)}) async-start(bf16[4,192,384]{2,1,0:T(8,128)(2,1)} %broadcast_in_dim.100), calls=%async_computation.11 | async-start | bytes 1179648 | tf_op jit(solution)/shard_map/all_to_all | solution.py:535
  248.1 5.7 %collective-permute-start.1 = (bf16[4,192,384]{2,1,0:T(8,128)(2,1)S(1)}, bf16[4,192,384]{2,1,0:T(8,128)(2,1)S(1)}, u32[]{:S(2)}, u32[]{:S(2)}) collective-permute-start(bf16[4,192,384]{2,1,0:T(8,128)(2,1)S(1)} %all-to-all-done.9.mine_ref), channel_id=1, source_target_pairs={{0,16},{16,0},{1,17},{17,1},{2,18},{18,2},{3,19},{19,3},{4,20},{20... | collective-permute-start | bytes 1769480 | tf_op jit(solution)/shard_map/ppermute | solution.py:547
  (15 other events, 48.3 us)
Sparse Core Ops, SparseCore 0:
  14.5 28.8 all-gather.7
  46.3 30.4 all-gather.9
  79.0 23.8 all-gather.5
  151.7 37.0 reduce-scatter.4
  202.6 22.2 reduce-scatter.2
